TPU v7x, 32 devices: a whole 2x2x4 slice. The times are simulated.
32 devices in a mesh: row: 8 (over y, x, core), col: 4 (over z).
Axes of the slice: x: 2, y: 2, z: 4, core: 2. Of those that a mesh axis runs over, the one named last changes fastest.
Arguments:
- hidden_states: bfloat16 [8192, 2048], P('row', 'col'), may hold values from -21 to 21
- lengths: int32 [16], P('row'), may hold values from 16 to 512, as said below
- qkvg_master: float32 [2048, 12288], P(('row', 'col')), may hold values from -0.125 to 0.125
- gateup_master: float32 [2, 2048, 4096], P(None, ('row', 'col')), may hold values from -0.125 to 0.125
- out_master: float32 [4096, 2048], P(None, ('row', 'col')), may hold values from -0.09375 to 0.09375
- down_master: float32 [4096, 2048], P(None, ('row', 'col')), may hold values from -0.09375 to 0.09375
Outputs:
- layer_output: bfloat16 [8192, 2048], P('row', 'col')
- qkvg_weight: bfloat16 [2048, 12288], P('row', 'col')
- gateup_weight: bfloat16 [2, 2048, 4096], P(None, 'row', 'col')
- mixing_weight: bfloat16 [4096, 2048], P('col', 'row')
- down_weight: bfloat16 [4096, 2048], P('col', 'row')
Inputs may be any that keep to these rules, and one draw needn't show every extreme that they name: `lengths`: prompt length of each request; the positions of a request from its length on are padding. Some request has length 512 in every draw.
All inputs are finite; a program needn't handle non-finite values.
Results may differ from a plain program's by a relative error of at most 0.014.
Values may be sent and summed in bfloat16 or wider, within the bound.
No kernel may reach another device: no remote copies, remote signals or barrier semaphores. Data moves between devices by JAX's collectives and lax.ppermute only.
A program may use at most 128 MiB of HBM per device.

v0:
```python
import functools
import math

import jax
import jax.numpy as jnp
from jax import lax
from jax.experimental import pallas as pl
from jax.experimental.pallas import tpu as pltpu
from jax.sharding import PartitionSpec as P

D = 2048
HEADS = 8
KEY = 256
VAL = 512
S = 512
TILE = 16
TILES = S // TILE
HEAD_WIDTH = 2 * KEY + 2 * VAL

epsilon = 1e-05
VMEM_LIMIT = 56 * 1024 * 1024

SMEM = pl.BlockSpec(memory_space=pltpu.SMEM)
VMEM = pl.BlockSpec(memory_space=pltpu.VMEM)
ANY = pl.BlockSpec(memory_space=pl.ANY)


def params():
    return pltpu.CompilerParams(vmem_limit_bytes=VMEM_LIMIT)


def cost(flops, moved):
    return pl.CostEstimate(flops=int(flops), bytes_accessed=int(moved), transcendentals=0)


def swap(block, axis, step):
    size = lax.axis_size(axis)
    return lax.ppermute(block, axis, [(i, i ^ step) for i in range(size)])


def after(value, *earlier):
    return lax.optimization_barrier((value,) + earlier)[0]


def gather_links(block, arrived=None, halves=(), whole=()):
    across, along = arrived or (swap(block, "row", 2), swap(block, "row", 4))
    pieces = {0: block, 2: across, 4: along}
    axis = block.ndim - 2
    half = block.shape[axis] // 2
    across, along = after((across, along), *halves)
    upper = swap(lax.slice_in_dim(along, 0, half, axis=axis), "row", 2)
    lower = swap(lax.slice_in_dim(across, half, 2 * half, axis=axis), "row", 4)
    pieces[6] = jnp.concatenate(after((upper, lower), *whole), axis=axis)
    return pieces


def gather_cores(pieces, earlier=()):
    own = pieces[0] if earlier else after(pieces[0], pieces[2], pieces[4])
    for j in (0, 2, 4, 6):
        pieces[j | 1] = swap(after(pieces[j], *earlier) if j else own, "row", 1)
    return [pieces[j] for j in range(8)]


def gather_rows(block, direct=False, **order):
    size = lax.axis_size("row")
    if size == 8 and not direct:
        return gather_cores(gather_links(block, **order))
    pieces = {0: block}
    if size == 8:
        for j in (2, 4, 6):
            pieces[j] = swap(block, "row", j)
        pieces[0] = after(block, pieces[2], pieces[4])
        bits = [1]
    else:
        bits = [1 << i for i in reversed(range(size.bit_length() - 1))]
    for bit in bits:
        for j in sorted(pieces):
            pieces[j | bit] = swap(pieces[j], "row", bit)
    return [pieces[j] for j in range(size)]


def last_parts(pieces):
    return (pieces[6],) if len(pieces) == 8 else (pieces[-1],)


def mark(block, lengths):
    digits = jnp.stack([lengths // TILE, lengths % TILE], axis=1).astype(jnp.bfloat16)
    rows = jnp.pad(digits, ((0, 2 * TILE - digits.shape[0]), (0, block.shape[1] - 2)))
    return jnp.concatenate([block, rows], axis=0)


def read_marks(pieces, per_row):
    rows = pieces[0].shape[0] - 2 * TILE
    digits = jnp.concatenate([piece[rows : rows + per_row, :2] for piece in pieces], axis=0).astype(jnp.int32)
    return digits[:, 0] * TILE + digits[:, 1]


def exchange(blocks):
    return [blocks[0]] + [swap(blocks[k], "col", k) for k in range(1, len(blocks))]


def gather_cols(block):
    size = lax.axis_size("col")
    if size != 4:
        return [(block,)] + [(swap(block, "col", k),) for k in range(1, size)]
    near = swap(block, "col", 1)
    far = swap(block, "col", 2)
    mine, passed = after((block, far), near)
    middle = lax.ppermute(mine, "col", [(1, 2), (2, 1)])
    ends = lax.ppermute(passed, "col", [(2, 3), (1, 0)])
    return [(block,), (near,), (far,), (middle, ends)]


def collect(terms, later=()):
    if lax.axis_size("col") != 4:
        parts = exchange(terms)
        return parts, parts[1:2]
    early = lax.ppermute(terms[3], "col", [(3, 2), (0, 1)])
    middle = lax.ppermute(terms[3], "col", [(1, 2), (2, 1)])
    term1, term2, early = after((terms[1], terms[2], early), middle, *later)
    near = swap(term1, "col", 1)
    both = term2.astype(jnp.float32) + early.astype(jnp.float32)
    far = swap(both.astype(jnp.bfloat16), "col", 2)
    return [terms[0], near, far, middle], (early, middle)


def added(parts):
    return sum(part.astype(jnp.float32) for part in parts)


def cut_front_kernel(cols, place, qkvg, out, *blocks):
    units = out.shape[1] // cols
    width = blocks[0].shape[1] - units
    for k in range(cols):
        target = lax.bitwise_xor(place[1], k)
        columns = pl.ds(pl.multiple_of(target * width, 128), width)
        blocks[k][:, :width] = qkvg[:, columns].astype(jnp.bfloat16)
        columns = pl.ds(pl.multiple_of(target * units, 128), units)
        blocks[k][:, width:] = out[:, columns].astype(jnp.bfloat16)


def cut_feed_kernel(cols, place, down, gateup, *blocks):
    units = blocks[0].shape[2]
    for k in range(cols):
        target = lax.bitwise_xor(place[1], k)
        columns = pl.ds(pl.multiple_of(target * units, 128), units)
        blocks[k][0] = down[:, columns].astype(jnp.bfloat16)
        blocks[k][1] = gateup[0, :, columns].astype(jnp.bfloat16)
        blocks[k][2] = gateup[1, :, columns].astype(jnp.bfloat16)


def cut(kernel, shape, place, *masters):
    cols = lax.axis_size("col")
    return pl.pallas_call(
        functools.partial(kernel, cols),
        out_shape=[jax.ShapeDtypeStruct(shape, jnp.bfloat16)] * cols,
        in_specs=[SMEM] + [VMEM] * len(masters),
        out_specs=[VMEM] * cols,
        compiler_params=params(),
        cost_estimate=cost(0, 6 * math.prod(shape) * cols),
    )(place, *masters)


def join_kernel(cols, place, *refs):
    out = refs[cols]
    rows = refs[0].shape[-2]
    for k in range(cols):
        source = lax.bitwise_xor(place[1], k)
        where = pl.ds(pl.multiple_of(source * rows, 16), rows)
        if len(out.shape) == 2:
            out[where, :] = refs[k][...]
        else:
            out[:, where, :] = refs[k][...]


def join(blocks, place):
    cols = len(blocks)
    shape = list(blocks[0].shape)
    shape[-2] *= cols
    return pl.pallas_call(
        functools.partial(join_kernel, cols),
        out_shape=jax.ShapeDtypeStruct(tuple(shape), jnp.bfloat16),
        in_specs=[SMEM] + [VMEM] * cols,
        out_specs=VMEM,
        compiler_params=params(),
        cost_estimate=cost(0, 4 * math.prod(shape)),
    )(place, *blocks)


def pack_kernel(requests, rows, passes, place, lengths, table, bins, starts, count, used):
    row = place[0]
    per_row = requests // rows

    def clear(i, carry):
        table[i] = -1
        return carry

    lax.fori_loop(0, passes * TILES, clear, 0)

    def clear_used(i, carry):
        used[i] = 0
        return carry

    lax.fori_loop(0, requests, clear_used, 0)

    def put(q, top):
        owner = q // per_row
        length = lengths[lax.bitwise_xor(owner, row) * per_row + (q - owner * per_row)]
        tiles = (length + (TILE - 1)) // TILE

        def look(i, best):
            b = requests - 1 - i
            return jnp.where(used[b] + tiles <= TILES, b, best)

        b = lax.fori_loop(0, requests, look, requests - 1)
        start = used[b]
        used[b] = start + tiles
        bins[q] = b
        starts[q] = start
        turn = b // rows

        @pl.when(b - turn * rows == row)
        def _():
            def note(i, carry):
                table[turn * TILES + start + i] = q * TILES + i
                return carry

            lax.fori_loop(0, tiles, note, 0)

        return jnp.maximum(top, b + 1)

    count[0] = lax.fori_loop(0, requests, put, 0)


def pack(place, lengths, rows):
    requests = lengths.shape[0]
    passes = requests // rows
    whole = lambda n: jax.ShapeDtypeStruct((n,), jnp.int32)
    return pl.pallas_call(
        functools.partial(pack_kernel, requests, rows, passes),
        out_shape=[whole(passes * TILES), whole(requests), whole(requests), whole(1)],
        in_specs=[SMEM, SMEM],
        out_specs=[SMEM] * 4,
        scratch_shapes=[pltpu.SMEM((requests,), jnp.int32)],
        compiler_params=params(),
    )(place, lengths)


def pick_kernel(rows, per_row, turn, place, table, *refs):
    pieces, out, sem = refs[:rows], refs[rows], refs[rows + 1]
    row = place[0]

    def step(i, carry):
        code = jnp.maximum(table[turn * TILES + i], 0)
        request = code // TILES
        owner = request // per_row
        tile = (request - owner * per_row) * TILES + (code - request * TILES)
        piece = lax.bitwise_xor(owner, row)
        source = pl.ds(pl.multiple_of(tile * TILE, TILE), TILE)
        target = pl.ds(pl.multiple_of(i * TILE, TILE), TILE)
        for j in range(rows):

            @pl.when(piece == j)
            def _():
                pltpu.make_async_copy(pieces[j].at[source, :], out.at[target, :], sem).start()

        return carry

    lax.fori_loop(0, TILES, step, 0)
    pltpu.make_async_copy(out, out, sem).wait()


def pick(place, table, pieces, turn):
    rows = len(pieces)
    width = pieces[0].shape[1]
    return pl.pallas_call(
        functools.partial(pick_kernel, rows, pieces[0].shape[0] // S, turn),
        out_shape=jax.ShapeDtypeStruct((S, width), jnp.bfloat16),
        in_specs=[SMEM, SMEM] + [ANY] * rows,
        out_specs=VMEM,
        scratch_shapes=[pltpu.SemaphoreType.DMA],
        compiler_params=params(),
        cost_estimate=cost(0, 4 * S * width),
    )(place, table, *pieces)


def spread_kernel(rows, per_row, total, place, lengths, bins, starts, *refs):
    pieces, out = refs[:total], refs[total]
    row = place[0]
    width = out.shape[1]
    for a in range(per_row):
        request = row * per_row + a
        length = lengths[a]
        b = bins[request]
        start = starts[request]
        turn = b // rows
        index = lax.bitwise_xor(b - turn * rows, row) + turn * rows
        tiles = (length + (TILE - 1)) // TILE

        def blank(i, carry):
            out[pl.ds(pl.multiple_of(a * S + i * TILE, TILE), TILE), :] = jnp.zeros((TILE, width), jnp.bfloat16)
            return carry

        lax.fori_loop(tiles, TILES, blank, 0)
        for j in range(total):

            @pl.when(index == j)
            def _():
                def move(i, carry):
                    values = pieces[j][pl.ds(pl.multiple_of((start + i) * TILE, TILE), TILE), :]
                    position = i * TILE + lax.broadcasted_iota(jnp.int32, (TILE, width), 0)
                    kept = jnp.where(position < length, values.astype(jnp.float32), 0.0)
                    out[pl.ds(pl.multiple_of(a * S + i * TILE, TILE), TILE), :] = kept.astype(jnp.bfloat16)
                    return carry

                lax.fori_loop(0, tiles, move, 0)


def spread(place, lengths, bins, starts, pieces, rows, per_row):
    width = pieces[0].shape[1]
    return pl.pallas_call(
        functools.partial(spread_kernel, rows, per_row, len(pieces)),
        out_shape=jax.ShapeDtypeStruct((per_row * S, width), jnp.bfloat16),
        in_specs=[SMEM] * 4 + [VMEM] * len(pieces),
        out_specs=VMEM,
        compiler_params=params(),
        cost_estimate=cost(0, 2 * S * width * (len(pieces) + per_row)),
    )(place, lengths, bins, starts, *pieces)


DOT = functools.partial(jnp.dot, preferred_element_type=jnp.float32)


def DOT_T(left, right):
    return lax.dot_general(left, right, (((1,), (1,)), ((), ())), preferred_element_type=jnp.float32)


def flatten(parts):
    return [part for entry in parts for part in entry], tuple(len(entry) for entry in parts)


def read_parts(refs, counts):
    at = 0
    for count in counts:
        block = refs[at][...]
        for other in refs[at + 1 : at + count]:
            block = block + other[...]
        at += count
        yield block


def silu(values):
    return values * (1.0 / (1.0 + jnp.exp(-values)))


def retain_kernel(rows, counts, heads, place, decays, cosine, sine, seg_col, seg_row, *refs):
    cols, number = len(counts), sum(counts)
    tokens, weights = refs[:number], refs[number : number + rows]
    mixed, normed, gathered, sems = refs[number + rows :]
    depth = D // rows
    width = D // cols
    parts = ((0, 2 * KEY), (2 * KEY, VAL), (2 * KEY + VAL, VAL))

    for head in range(heads):
        for i, (low, size) in enumerate(parts):
            columns = pl.ds(head * HEAD_WIDTH + low, size)
            for j in range(rows):
                where = pl.ds(pl.multiple_of(lax.bitwise_xor(place[0], j) * depth, depth), depth)
                pltpu.make_async_copy(
                    weights[j].at[:, columns], gathered.at[where, columns], sems.at[head * 3 + i]
                ).start()

    total = jnp.zeros((S, 1), jnp.float32)
    for block in read_parts(tokens, counts):
        values = block.astype(jnp.float32)
        total += jnp.sum(values * values, axis=1, keepdims=True)
    scale = lax.rsqrt(total / D + epsilon)
    for k, block in enumerate(read_parts(tokens, counts)):
        where = pl.ds(pl.multiple_of(lax.bitwise_xor(place[1], k) * width, width), width)
        normed[:, where] = (block.astype(jnp.float32) * scale).astype(jnp.bfloat16)

    def project(head, i):
        low, size = parts[i]
        columns = pl.ds(head * HEAD_WIDTH + low, size)
        view = gathered.at[:, columns]
        pltpu.make_async_copy(view, view, sems.at[head * 3 + i]).wait()
        return DOT(normed[...], gathered[:, columns]).astype(jnp.bfloat16)

    def rotate(values):
        values = values.astype(jnp.float32)
        first, second = values[:, : KEY // 2], values[:, KEY // 2 :]
        cos, sin = cosine[...], sine[...]
        return jnp.concatenate([first * cos - second * sin, first * sin + second * cos], axis=1)

    lag = lax.broadcasted_iota(jnp.int32, (S, S), 0) - lax.broadcasted_iota(jnp.int32, (S, S), 1)
    allowed = (lag >= 0) & (seg_col[...] == seg_row[...])
    span = jnp.where(allowed, lag.astype(jnp.float32), 1e6)
    for head in range(heads):
        both = project(head, 0)
        query = rotate(both[:, :KEY]).astype(jnp.bfloat16)
        keyed = (rotate(both[:, KEY:]) * (1.0 / math.sqrt(KEY))).astype(jnp.bfloat16)
        scores = DOT_T(query, keyed)
        scores = scores * jnp.exp(span * decays[head])
        denom = jnp.sum(scores, axis=1, keepdims=True)
        value = project(head, 1)
        retained = DOT(scores.astype(jnp.bfloat16), value) / jnp.maximum(jnp.abs(denom), 1.0)
        centred = retained - jnp.mean(retained, axis=1, keepdims=True)
        spread_of = jnp.mean(centred * centred, axis=1, keepdims=True)
        grouped = centred * lax.rsqrt(spread_of + epsilon)
        gate = project(head, 2).astype(jnp.float32)
        mixed[:, head * VAL : (head + 1) * VAL] = (silu(gate) * grouped).astype(jnp.bfloat16)


def retain(place, decays, cosine, sine, seg_col, seg_row, tokens, weights):
    rows, cols = len(weights), len(tokens)
    heads = HEADS // cols
    flat, counts = flatten(tokens)
    return pl.pallas_call(
        functools.partial(retain_kernel, rows, counts, heads),
        out_shape=jax.ShapeDtypeStruct((S, heads * VAL), jnp.bfloat16),
        in_specs=[SMEM, SMEM] + [VMEM] * (4 + len(flat)) + [ANY] * rows,
        out_specs=VMEM,
        scratch_shapes=[
            pltpu.VMEM((S, D), jnp.bfloat16),
            pltpu.VMEM((D, heads * HEAD_WIDTH), jnp.bfloat16),
            pltpu.SemaphoreType.DMA((heads * 3,)),
        ],
        compiler_params=params(),
        cost_estimate=cost(2 * S * D * HEAD_WIDTH * heads * 1.3, 2 * D * HEAD_WIDTH * heads),
    )(place, decays, cosine, sine, seg_col, seg_row, *flat, *weights)


def load_terms(rows, cols, place, views, gathered, sem):
    ratio = rows // cols
    for j in range(rows):
        owner = lax.bitwise_xor(place[0], j)
        target = owner // ratio
        slot = lax.bitwise_xor(target, place[1]) * ratio + (owner - target * ratio)
        pltpu.make_async_copy(views[j], gathered.at[slot], sem).start()


def put_terms(rows, cols, left, gathered, sem, outs):
    ratio = rows // cols
    depth = D // rows
    pltpu.make_async_copy(gathered, gathered, sem).wait()
    for slot in range(rows):
        k, i = slot // ratio, slot % ratio
        outs[k][:, i * depth : (i + 1) * depth] = DOT_T(left, gathered[slot]).astype(jnp.bfloat16)


def mix_kernel(rows, cols, place, mixed, *refs):
    weights, outs = refs[:rows], refs[rows : rows + cols]
    gathered, sem = refs[rows + cols :]
    units = mixed.shape[1]
    views = [ref.at[:, pl.ds(ref.shape[1] - units, units)] for ref in weights]
    load_terms(rows, cols, place, views, gathered, sem)
    put_terms(rows, cols, mixed[...], gathered, sem, outs)


def mix(place, mixed, weights, cols):
    rows = len(weights)
    width = D // cols
    return pl.pallas_call(
        functools.partial(mix_kernel, rows, cols),
        out_shape=[jax.ShapeDtypeStruct((S, width), jnp.bfloat16)] * cols,
        in_specs=[SMEM, VMEM] + [ANY] * rows,
        out_specs=[VMEM] * cols,
        scratch_shapes=[
            pltpu.VMEM((rows, D // rows, mixed.shape[1]), jnp.bfloat16),
            pltpu.SemaphoreType.DMA,
        ],
        compiler_params=params(),
        cost_estimate=cost(2 * S * D * mixed.shape[1], 2 * D * mixed.shape[1]),
    )(place, mixed, *weights)


def feed_kernel(rows, counts, tile, place, *refs):
    cols, number = len(counts), sum(counts)
    tokens = refs[:number]
    weights = refs[number : number + rows]
    outs = refs[number + rows : number + rows + cols]
    ordered, hidden, gathered, gathered_down, sems, sem_down = refs[number + rows + cols :]
    depth = D // rows
    width = D // cols
    steps = gathered.shape[2] // tile

    for step in range(steps):
        columns = pl.ds(step * tile, tile)
        for j in range(rows):
            where = pl.ds(pl.multiple_of(lax.bitwise_xor(place[0], j) * depth, depth), depth)
            pltpu.make_async_copy(
                weights[j].at[pl.ds(1, 2), :, columns], gathered.at[:, where, columns], sems.at[step]
            ).start()
    load_terms(rows, cols, place, [ref.at[0] for ref in weights], gathered_down, sem_down)

    total = jnp.zeros((S, 1), jnp.float32)
    for k, block in enumerate(read_parts(tokens, counts)):
        values = block.astype(jnp.float32)
        total += jnp.sum(values * values, axis=1, keepdims=True)
        where = pl.ds(pl.multiple_of(lax.bitwise_xor(place[1], k) * width, width), width)
        ordered[:, where] = block
    scale = lax.rsqrt(total / D + epsilon)

    for step in range(steps):
        columns = pl.ds(step * tile, tile)
        view = gathered.at[:, :, columns]
        pltpu.make_async_copy(view, view, sems.at[step]).wait()
        gate = DOT(ordered[...], gathered[0, :, columns]) * scale
        up = DOT(ordered[...], gathered[1, :, columns]) * scale
        hidden[:, columns] = (silu(gate) * up).astype(jnp.bfloat16)
    put_terms(rows, cols, hidden[...], gathered_down, sem_down, outs)


def feed(place, tokens, weights):
    rows, cols = len(weights), len(tokens)
    units = weights[0].shape[2]
    tile = min(units, 512)
    flat, counts = flatten(tokens)
    return pl.pallas_call(
        functools.partial(feed_kernel, rows, counts, tile),
        out_shape=[jax.ShapeDtypeStruct((S, D // cols), jnp.bfloat16)] * cols,
        in_specs=[SMEM] + [VMEM] * len(flat) + [ANY] * rows,
        out_specs=[VMEM] * cols,
        scratch_shapes=[
            pltpu.VMEM((S, D), jnp.bfloat16),
            pltpu.VMEM((S, units), jnp.bfloat16),
            pltpu.VMEM((2, D, units), jnp.bfloat16),
            pltpu.VMEM((rows, D // rows, units), jnp.bfloat16),
            pltpu.SemaphoreType.DMA((units // tile,)),
            pltpu.SemaphoreType.DMA,
        ],
        compiler_params=params(),
        cost_estimate=cost(6 * S * D * units, 6 * D * units),
    )(place, *flat, *weights)


def shards(hidden_states, lengths, qkvg_master, gateup_master, out_master, down_master):
    rows, cols = lax.axis_size("row"), lax.axis_size("col")
    per_row = lengths.shape[0]
    heads = HEADS // cols
    place = jnp.stack([lax.axis_index("row"), lax.axis_index("col")]).astype(jnp.int32)

    depth = qkvg_master.shape[0]
    units = gateup_master.shape[2] // cols
    width = heads * HEAD_WIDTH
    front_cut = cut(cut_front_kernel, (depth, width + units), place, qkvg_master, out_master.T)
    front_parts = exchange(front_cut)
    marked = mark(hidden_states, lengths)
    everyone = gather_rows(after(marked, front_cut[0]), halves=front_parts[1:3])
    front_blocks = join(front_parts, place)
    feed_cut = cut(cut_feed_kernel, (3, depth, units), place, down_master.T, gateup_master)
    all_lengths = read_marks(everyone, per_row)

    table, bins, starts, count = pack(place, all_lengths, rows)

    head_ids = lax.axis_index("col") * heads + jnp.arange(heads)
    decays = jnp.log1p(-jnp.power(2.0, -5.0 - head_ids.astype(jnp.float32)))
    freq = jnp.power(10000.0, -2.0 * jnp.arange(KEY // 2).astype(jnp.float32) / KEY)

    def begin(turn):
        codes = table[turn * TILES : (turn + 1) * TILES]
        segments = jnp.where(codes < 0, -1, codes // TILES)
        seg = jnp.broadcast_to(segments[:, None], (TILES, TILE)).reshape(S)
        positions = ((jnp.maximum(codes, 0) % TILES)[:, None] * TILE + jnp.arange(TILE)[None, :]).reshape(S)
        angle = positions.astype(jnp.float32)[:, None] * freq[None, :]
        own = pick(place, table, everyone, turn)
        return own, (jnp.cos(angle), jnp.sin(angle), seg[:, None], seg[None, :])

    own, tables = begin(0)
    tokens = gather_cols(own)
    ahead = [tokens[1][0], tokens[2][0]]
    rest = [part for entry in tokens[3:] for part in entry]
    feed_parts = exchange(list(after(tuple(feed_cut), *rest)))
    front_pieces = gather_rows(
        after(front_blocks, *last_parts(everyone)), halves=ahead, whole=(*rest, *tables, *feed_parts[1:])
    )

    mixed = retain(place, decays, *tables, tokens, front_pieces)
    terms = mix(place, mixed, front_pieces, cols)
    feed_blocks = after(join(feed_parts, place), *last_parts(front_pieces))
    whole = rows == 8
    arrived = (swap(feed_blocks, "row", 2), swap(feed_blocks, "row", 4)) if whole else ()
    attended, early = collect(terms, later=arrived)
    residual = own.astype(jnp.float32) + added(attended)
    sent = residual.astype(jnp.bfloat16)
    if whole:
        links = gather_links(feed_blocks, arrived=arrived, halves=early)
        mid_tokens = gather_cols(after(sent, links[6]))
        feed_pieces = gather_cores(links, earlier=(mid_tokens[1][0], mid_tokens[2][0]))
    else:
        mid_tokens = gather_cols(sent)
        feed_pieces = gather_rows(feed_blocks)

    weights = (front_blocks[:, :width], feed_blocks[1:], front_blocks[:, width:].T, feed_blocks[0].T)
    weights = lax.optimization_barrier(weights)

    def rest_of_layer(residual, tokens, feed_pieces):
        fed, _ = collect(feed(place, tokens, feed_pieces))
        return gather_rows((residual + added(fed)).astype(jnp.bfloat16), direct=True)

    first = rest_of_layer(residual, mid_tokens, [after(feed_pieces[0], *weights)] + feed_pieces[1:])

    def finish(pieces):
        return spread(place, lengths, bins, starts, pieces, rows, per_row)

    def more(pieces):
        for turn in range(1, per_row):
            own, tables = begin(turn)
            mixed = retain(place, decays, *tables, gather_cols(own), front_pieces)
            attended, _ = collect(mix(place, mixed, front_pieces, cols))
            residual = own.astype(jnp.float32) + added(attended)
            pieces = pieces + rest_of_layer(residual, gather_cols(residual.astype(jnp.bfloat16)), feed_pieces)
        return finish(pieces)

    layer_output = lax.cond(count[0] > rows, more, finish, first)
    return (layer_output,) + weights


def solution(mesh):
    return jax.shard_map(
        shards,
        mesh=mesh,
        in_specs=(
            P("row", "col"),
            P("row"),
            P(("row", "col"), None),
            P(None, ("row", "col"), None),
            P(None, ("row", "col")),
            P(None, ("row", "col")),
        ),
        out_specs=(
            P("row", "col"),
            P("row", "col"),
            P(None, "row", "col"),
            P("col", "row"),
            P("col", "row"),
        ),
        check_vma=False,
    )
```

profile of v0, /device:TPU:0, one launch (start us, length us, event | category | flops | bytes accessed | tf_op | source)
XLA Modules:
  0.0 382.8 jit_solution(10337905582335043824)
XLA Ops:
  3.0 3.7 shard_map.101
  6.7 3.0 collective-permute-start.24
  15.3 18.2 %collective-permute-done.24.refs_4_ = bf16[1056,512]{1,0:T(8,128)(2,1)S(1)} collective-permute-done((bf16[1056,512]{1,0:T(8,128)(2,1)S(1)}, bf16[1056,512]{1,0:T(8,128)(2,1)S(1)}, u32[]{:S(2)}, u32[]{:S(2)}) %collective-permute-start.24) | collective-permute-done | bytes 1081376 | tf_op jit(solution)/shard_map/ppermute | solution.py:38
  42.8 11.3 %collective-permute-done.37.refs_3_ = bf16[64,4096]{1,0:T(8,128)(2,1)} collective-permute-done((bf16[64,4096]{1,0:T(8,128)(2,1)S(1)}, bf16[64,4096]{1,0:T(8,128)(2,1)}, u32[]{:S(2)}, u32[]{:S(2)}) %collective-permute-start.37) | collective-permute-done | bytes 524320 | tf_op jit(solution)/shard_map/ppermute | solution.py:38
  66.4 4.1 %shard_map.102 = (s32[64]{0:T(128)S(1)}, s32[16]{0:T(128)S(1)}, s32[16]{0:T(128)S(1)}, s32[1]{0:T(128)}) custom-call(s32[2]{0:T(128)S(1)} %pad_add_fusion.place, s32[16]{0:T(128)} %add_bitcast_fusion.lengths), custom_call_target="tpu_custom_call" | custom-call | tf_op jit(solution)/shard_map/pallas_call | solution.py:239
  70.5 3.2 shard_map.103.refs_0_
  73.8 11.9 %collective-permute-start.34 = (bf16[512,512]{1,0:T(8,128)(2,1)}, bf16[512,512]{1,0:T(8,128)(2,1)}, u32[]{:S(2)}, u32[]{:S(2)}) collective-permute-start(bf16[512,512]{1,0:T(8,128)(2,1)} %shard_map.103.refs_0_), channel_id=1, source_target_pairs={{0,2},{1,3},{2,0},{3,1},{4,6},{5,7},{6,4},{7,5},{8,10},{9,11},{10,... | collective-permute-start | bytes 1572872 | tf_op jit(solution)/shard_map/ppermute | solution.py:38
  85.7 24.1 %collective-permute-done.34.refs_2_ = bf16[512,512]{1,0:T(8,128)(2,1)} collective-permute-done((bf16[512,512]{1,0:T(8,128)(2,1)}, bf16[512,512]{1,0:T(8,128)(2,1)}, u32[]{:S(2)}, u32[]{:S(2)}) %collective-permute-start.34) | collective-permute-done | bytes 524320 | tf_op jit(solution)/shard_map/ppermute | solution.py:38
  121.2 3.2 shard_map.105
  125.3 10.9 %collective-permute-done.36.refs_4_ = bf16[512,512]{1,0:T(8,128)(2,1)} collective-permute-done((bf16[512,512]{1,0:T(8,128)(2,1)}, bf16[512,512]{1,0:T(8,128)(2,1)}, u32[]{:S(2)}, u32[]{:S(2)}) %collective-permute-start.36) | collective-permute-done | bytes 524320 | tf_op jit(solution)/shard_map/ppermute | solution.py:110
  136.6 2.8 collective-permute-start.46
  142.6 8.5 %collective-permute-done.45.refs_1_ = bf16[3,64,1024]{2,1,0:T(8,128)(2,1)} collective-permute-done((bf16[3,64,1024]{2,1,0:T(8,128)(2,1)}, bf16[3,64,1024]{2,1,0:T(8,128)(2,1)}, u32[]{:S(2)}, u32[]{:S(2)}) %collective-permute-start.45) | collective-permute-done | bytes 393248 | tf_op jit(solution)/shard_map/ppermute | solution.py:38
  151.1 15.7 %collective-permute-done.46.refs_2_ = bf16[3,64,1024]{2,1,0:T(8,128)(2,1)} collective-permute-done((bf16[3,64,1024]{2,1,0:T(8,128)(2,1)}, bf16[3,64,1024]{2,1,0:T(8,128)(2,1)}, u32[]{:S(2)}, u32[]{:S(2)}) %collective-permute-start.46) | collective-permute-done | bytes 393248 | tf_op jit(solution)/shard_map/ppermute | solution.py:38
  171.9 2.6 shard_map.108.refs_5_
  177.3 14.2 %shard_map.106.mixed = bf16[512,1024]{1,0:T(8,128)(2,1)} custom-call(s32[2]{0:T(128)S(1)} %pad_add_fusion.place, f32[2]{0:T(128)S(1)} %negate_log-plus-one_fusion.decays, f32[512,128]{1,0:T(8,128)} %get-tuple-element.328.cosine, f32[512,128]{1,0:T(8,128)} %get-tuple-element.327.sine, s32[512,1]{1,0:T(8,128)} %copy.32.seg_col, ...), custom_call_target="tpu_custom_call" | custom-call | flops 8375186432 | bytes 12582912 | tf_op jit(solution)/shard_map/pallas_call | solution.py:418
  191.5 6.5 %shard_map.107 = (bf16[512,512]{1,0:T(8,128)(2,1)}, bf16[512,512]{1,0:T(8,128)(2,1)}, bf16[512,512]{1,0:T(8,128)(2,1)}, bf16[512,512]{1,0:T(8,128)(2,1)}) custom-call(s32[2]{0:T(128)S(1)} %pad_add_fusion.place, bf16[512,1024]{1,0:T(8,128)(2,1)} %shard_map.106.mixed, bf16[256,4096]{1,0:T(8,128)(2,1)S(1)} %shard_map.104.refs_5_.refs_0_, ...), custom_call_target="tpu_custom_call" | custom-call | flops 2147483648 | bytes 4194304 | tf_op jit(solution)/shard_map/pallas_call | solution.py:463
  198.8 9.7 %collective-permute-start.49 = (bf16[512,512]{1,0:T(8,128)(2,1)}, bf16[512,512]{1,0:T(8,128)(2,1)S(1)}, u32[]{:S(2)}, u32[]{:S(2)}) collective-permute-start(bf16[512,512]{1,0:T(8,128)(2,1)} %get-tuple-element.279), channel_id=1, source_target_pairs={{3,2},{0,1},{7,6},{4,5},{11,10},{8,9},{15,14},{12,13},{19,18},{16,... | collective-permute-start | bytes 1572872 | tf_op jit(solution)/shard_map/ppermute | solution.py:118
  208.5 3.1 collective-permute-done.52.refs_9_
  212.8 6.4 %collective-permute-done.49 = bf16[512,512]{1,0:T(8,128)(2,1)S(1)} collective-permute-done((bf16[512,512]{1,0:T(8,128)(2,1)}, bf16[512,512]{1,0:T(8,128)(2,1)S(1)}, u32[]{:S(2)}, u32[]{:S(2)}) %collective-permute-start.49) | collective-permute-done | bytes 524320 | tf_op jit(solution)/shard_map/ppermute | solution.py:118
  227.9 16.9 %collective-permute-done.54 = bf16[512,512]{1,0:T(8,128)(2,1)S(1)} collective-permute-done((bf16[512,512]{1,0:T(8,128)(2,1)S(1)}, bf16[512,512]{1,0:T(8,128)(2,1)S(1)}, u32[]{:S(2)}, u32[]{:S(2)}) %collective-permute-start.54) | collective-permute-done | bytes 524320 | tf_op jit(solution)/shard_map/ppermute | solution.py:38
  249.3 21.3 %collective-permute-done.58.refs_2_ = bf16[512,512]{1,0:T(8,128)(2,1)S(1)} collective-permute-done((bf16[512,512]{1,0:T(8,128)(2,1)S(1)}, bf16[512,512]{1,0:T(8,128)(2,1)S(1)}, u32[]{:S(2)}, u32[]{:S(2)}) %collective-permute-start.58) | collective-permute-done | bytes 524320 | tf_op jit(solution)/shard_map/ppermute | solution.py:38
  279.6 8.6 %collective-permute-done.60.refs_4_ = bf16[512,512]{1,0:T(8,128)(2,1)S(1)} collective-permute-done((bf16[512,512]{1,0:T(8,128)(2,1)S(1)}, bf16[512,512]{1,0:T(8,128)(2,1)S(1)}, u32[]{:S(2)}, u32[]{:S(2)}) %collective-permute-start.60) | collective-permute-done | bytes 524320 | tf_op jit(solution)/shard_map/ppermute | solution.py:110
  289.0 11.7 %shard_map.109 = (bf16[512,512]{1,0:T(8,128)(2,1)}, bf16[512,512]{1,0:T(8,128)(2,1)}, bf16[512,512]{1,0:T(8,128)(2,1)}, bf16[512,512]{1,0:T(8,128)(2,1)}) custom-call(s32[2]{0:T(128)S(1)} %pad_add_fusion.place, bf16[512,512]{1,0:T(8,128)(2,1)} %copy-done.18, bf16[512,512]{1,0:T(8,128)(2,1)} %copy-done.25, bf16[512,512]{1,0:T(8,128)(2,1)} %copy-done.24, ...), custom_call_target="tpu_custom_call" | custom-call | flops 6442450944 | bytes 12582912 | tf_op jit(solution)/shard_map/pallas_call | solution.py:519
  301.6 4.5 %collective-permute-start.65 = (bf16[512,512]{1,0:T(8,128)(2,1)}, bf16[512,512]{1,0:T(8,128)(2,1)S(1)}, u32[]{:S(2)}, u32[]{:S(2)}) collective-permute-start(bf16[512,512]{1,0:T(8,128)(2,1)} %get-tuple-element.303), channel_id=1, source_target_pairs={{3,2},{0,1},{7,6},{4,5},{11,10},{8,9},{15,14},{12,13},{19,18},{16,... | collective-permute-start | bytes 1572872 | tf_op jit(solution)/shard_map/ppermute | solution.py:118
  306.1 11.0 %collective-permute-done.65 = bf16[512,512]{1,0:T(8,128)(2,1)S(1)} collective-permute-done((bf16[512,512]{1,0:T(8,128)(2,1)}, bf16[512,512]{1,0:T(8,128)(2,1)S(1)}, u32[]{:S(2)}, u32[]{:S(2)}) %collective-permute-start.65) | collective-permute-done | bytes 524320 | tf_op jit(solution)/shard_map/ppermute | solution.py:118
  318.3 3.4 collective-permute-start.68
  321.7 22.0 %collective-permute-done.68 = bf16[512,512]{1,0:T(8,128)(2,1)S(1)} collective-permute-done((bf16[512,512]{1,0:T(8,128)(2,1)S(1)}, bf16[512,512]{1,0:T(8,128)(2,1)S(1)}, u32[]{:S(2)}, u32[]{:S(2)}) %collective-permute-start.68) | collective-permute-done | bytes 524320 | tf_op jit(solution)/shard_map/ppermute | solution.py:38
  349.7 10.8 %collective-permute-done.70 = bf16[512,512]{1,0:T(8,128)(2,1)} collective-permute-done((bf16[512,512]{1,0:T(8,128)(2,1)}, bf16[512,512]{1,0:T(8,128)(2,1)}, u32[]{:S(2)}, u32[]{:S(2)}) %collective-permute-start.70) | collective-permute-done | bytes 524320 | tf_op jit(solution)/shard_map/ppermute | solution.py:38
  360.5 2.9 collective-permute-done.69
  363.4 8.3 %collective-permute-done.74 = bf16[512,512]{1,0:T(8,128)(2,1)} collective-permute-done((bf16[512,512]{1,0:T(8,128)(2,1)}, bf16[512,512]{1,0:T(8,128)(2,1)}, u32[]{:S(2)}, u32[]{:S(2)}) %collective-permute-start.74) | collective-permute-done | bytes 524320 | tf_op jit(solution)/shard_map/ppermute | solution.py:38
  377.0 4.5 %conditional.1 = (bf16[1024,512]{1,0:T(8,128)(2,1)}) conditional(s32[]{:T(128)} %bitcast.6, (s32[2]{0:T(128)S(1)}, s32[2]{0:T(128)S(1)}, s32[16]{0:T(128)S(1)}, s32[16]{0:T(128)S(1)}, bf16[512,512]{1,0:T(8,128)(2,1)}, /*index=5*/bf16[512,512]{1,0:T(8,128)(2,1)}, bf16[512,512]{1,0:T(8,128)(2,1)}, bf16[512,512]{1,0:T(8,128)(2,1)}, ...), branch_computations={%region_0.1_spmd, %region_1.2_spmd} | conditional | flops 16974625792 | bytes 148395584 | solution.py:615
  377.0 3.6 branch_0_fun.1
  (179 shorter events, 90.7 us)
Async XLA Ops:
  6.7 26.8 %collective-permute-start.24 = (bf16[1056,512]{1,0:T(8,128)(2,1)S(1)}, bf16[1056,512]{1,0:T(8,128)(2,1)S(1)}, u32[]{:S(2)}, u32[]{:S(2)}) collective-permute-start(bf16[1056,512]{1,0:T(8,128)(2,1)S(1)} %pad_maximum_fusion.refs_0_), channel_id=1, source_target_pairs={{0,16},{4,20},{8,24},{12,28},{16,0},{20,4},{24,8},{28,12},{1,17},{... | collective-permute-start | bytes 3244040 | tf_op jit(solution)/shard_map/ppermute | solution.py:38
  9.6 28.3 %collective-permute-start.23 = (bf16[1056,512]{1,0:T(8,128)(2,1)S(1)}, bf16[1056,512]{1,0:T(8,128)(2,1)}, u32[]{:S(2)}, u32[]{:S(2)}) collective-permute-start(bf16[1056,512]{1,0:T(8,128)(2,1)S(1)} %pad_maximum_fusion.refs_0_), channel_id=1, source_target_pairs={{0,8},{4,12},{8,0},{12,4},{16,24},{20,28},{24,16},{28,20},{1,9},{5... | collective-permute-start | bytes 3244040 | tf_op jit(solution)/shard_map/ppermute | solution.py:38
  11.1 24.4 %collective-permute-start.28 = (bf16[64,4096]{1,0:T(8,128)(2,1)}, bf16[64,4096]{1,0:T(8,128)(2,1)S(1)}, u32[]{:S(2)}, u32[]{:S(2)}) collective-permute-start(bf16[64,4096]{1,0:T(8,128)(2,1)} %get-tuple-element.250), channel_id=1, source_target_pairs={{0,1},{1,0},{2,3},{3,2},{4,5},{5,4},{6,7},{7,6},{8,9},{9,8},{10,11... | collective-permute-start | bytes 1572872 | tf_op jit(solution)/shard_map/ppermute | solution.py:38
  12.7 25.2 %collective-permute-start.29 = (bf16[64,4096]{1,0:T(8,128)(2,1)}, bf16[64,4096]{1,0:T(8,128)(2,1)S(1)}, u32[]{:S(2)}, u32[]{:S(2)}) collective-permute-start(bf16[64,4096]{1,0:T(8,128)(2,1)} %get-tuple-element.251), channel_id=1, source_target_pairs={{0,2},{1,3},{2,0},{3,1},{4,6},{5,7},{6,4},{7,5},{8,10},{9,11},{10,... | collective-permute-start | bytes 1572872 | tf_op jit(solution)/shard_map/ppermute | solution.py:38
  33.5 25.7 %collective-permute-start.27 = (bf16[1056,512]{1,0:T(8,128)(2,1)S(1)}, bf16[1056,512]{1,0:T(8,128)(2,1)S(1)}, u32[]{:S(2)}, u32[]{:S(2)}) collective-permute-start(bf16[1056,512]{1,0:T(8,128)(2,1)S(1)} %collective-permute-done.24.refs_4_), channel_id=1, source_target_pairs={{0,4},{4,0},{8,12},{12,8},{16,20},{20,16},{24,28},{28,24},{1,5},{5... | collective-permute-start | bytes 3244040 | tf_op jit(solution)/shard_map/ppermute | solution.py:38
  39.2 16.6 %collective-permute-start.31 = (bf16[528,512]{1,0:T(8,128)(2,1)S(1)}, bf16[528,512]{1,0:T(8,128)(2,1)S(1)}, u32[]{:S(2)}, u32[]{:S(2)}) collective-permute-start(bf16[528,512]{1,0:T(8,128)(2,1)S(1)} %slice.73), channel_id=1, source_target_pairs={{0,16},{4,20},{8,24},{12,28},{16,0},{20,4},{24,8},{28,12},{1,17},{... | collective-permute-start | bytes 1622024 | tf_op jit(solution)/shard_map/ppermute | solution.py:38
  57.6 52.2 %collective-permute-start.39 = (bf16[256,4096]{1,0:T(8,128)(2,1)S(1)}, bf16[256,4096]{1,0:T(8,128)(2,1)}, u32[]{:S(2)}, u32[]{:S(2)}) collective-permute-start(bf16[256,4096]{1,0:T(8,128)(2,1)S(1)} %shard_map.104.refs_5_.refs_0_), channel_id=1, source_target_pairs={{0,16},{4,20},{8,24},{12,28},{16,0},{20,4},{24,8},{28,12},{1,17},{... | collective-permute-start | bytes 6291464 | tf_op jit(solution)/shard_map/ppermute | solution.py:38
  58.1 52.5 %collective-permute-start.38 = (bf16[256,4096]{1,0:T(8,128)(2,1)S(1)}, bf16[256,4096]{1,0:T(8,128)(2,1)}, u32[]{:S(2)}, u32[]{:S(2)}) collective-permute-start(bf16[256,4096]{1,0:T(8,128)(2,1)S(1)} %shard_map.104.refs_5_.refs_0_), channel_id=1, source_target_pairs={{0,8},{4,12},{8,0},{12,4},{16,24},{20,28},{24,16},{28,20},{1,9},{5... | collective-permute-start | bytes 6291464 | tf_op jit(solution)/shard_map/ppermute | solution.py:38
  73.8 36.0 %collective-permute-start.34 = (bf16[512,512]{1,0:T(8,128)(2,1)}, bf16[512,512]{1,0:T(8,128)(2,1)}, u32[]{:S(2)}, u32[]{:S(2)}) collective-permute-start(bf16[512,512]{1,0:T(8,128)(2,1)} %shard_map.103.refs_0_), channel_id=1, source_target_pairs={{0,2},{1,3},{2,0},{3,1},{4,6},{5,7},{6,4},{7,5},{8,10},{9,11},{10,... | collective-permute-start | bytes 1572872 | tf_op jit(solution)/shard_map/ppermute | solution.py:38
  85.7 24.1 %collective-permute-start.33 = (bf16[512,512]{1,0:T(8,128)(2,1)}, bf16[512,512]{1,0:T(8,128)(2,1)S(1)}, u32[]{:S(2)}, u32[]{:S(2)}) collective-permute-start(bf16[512,512]{1,0:T(8,128)(2,1)} %shard_map.103.refs_0_), channel_id=1, source_target_pairs={{0,1},{1,0},{2,3},{3,2},{4,5},{5,4},{6,7},{7,6},{8,9},{9,8},{10,11... | collective-permute-start | bytes 1572872 | tf_op jit(solution)/shard_map/ppermute | solution.py:38
  115.1 52.1 %collective-permute-start.44 = (bf16[128,4096]{1,0:T(8,128)(2,1)}, bf16[128,4096]{1,0:T(8,128)(2,1)}, u32[]{:S(2)}, u32[]{:S(2)}) collective-permute-start(bf16[128,4096]{1,0:T(8,128)(2,1)} %slice.80), channel_id=1, source_target_pairs={{0,16},{4,20},{8,24},{12,28},{16,0},{20,4},{24,8},{28,12},{1,17},{... | collective-permute-start | bytes 3145736 | tf_op jit(solution)/shard_map/ppermute | solution.py:38
  116.8 50.5 %collective-permute-start.43 = (bf16[128,4096]{1,0:T(8,128)(2,1)}, bf16[128,4096]{1,0:T(8,128)(2,1)}, u32[]{:S(2)}, u32[]{:S(2)}) collective-permute-start(bf16[128,4096]{1,0:T(8,128)(2,1)} %slice.79), channel_id=1, source_target_pairs={{0,8},{4,12},{8,0},{12,4},{16,24},{20,28},{24,16},{28,20},{1,9},{5... | collective-permute-start | bytes 3145736 | tf_op jit(solution)/shard_map/ppermute | solution.py:38
  119.7 16.5 %collective-permute-start.36 = (bf16[512,512]{1,0:T(8,128)(2,1)}, bf16[512,512]{1,0:T(8,128)(2,1)}, u32[]{:S(2)}, u32[]{:S(2)}) collective-permute-start(bf16[512,512]{1,0:T(8,128)(2,1)} %collective-permute-done.34.refs_2_), channel_id=1, source_target_pairs={{2,3},{1,0},{6,7},{5,4},{10,11},{9,8},{14,15},{13,12},{18,19},{17,... | collective-permute-start | bytes 1572872 | tf_op jit(solution)/shard_map/ppermute | solution.py:110
  136.6 30.1 %collective-permute-start.46 = (bf16[3,64,1024]{2,1,0:T(8,128)(2,1)}, bf16[3,64,1024]{2,1,0:T(8,128)(2,1)}, u32[]{:S(2)}, u32[]{:S(2)}) collective-permute-start(bf16[3,64,1024]{2,1,0:T(8,128)(2,1)} %get-tuple-element.272), channel_id=1, source_target_pairs={{0,2},{1,3},{2,0},{3,1},{4,6},{5,7},{6,4},{7,5},{8,10},{9,11},{10,... | collective-permute-start | bytes 1179656 | tf_op jit(solution)/shard_map/ppermute | solution.py:38
  139.4 27.4 %collective-permute-start.47 = (bf16[3,64,1024]{2,1,0:T(8,128)(2,1)}, bf16[3,64,1024]{2,1,0:T(8,128)(2,1)}, u32[]{:S(2)}, u32[]{:S(2)}) collective-permute-start(bf16[3,64,1024]{2,1,0:T(8,128)(2,1)} %get-tuple-element.273), channel_id=1, source_target_pairs={{0,3},{1,2},{2,1},{3,0},{4,7},{5,6},{6,5},{7,4},{8,11},{9,10},{10,... | collective-permute-start | bytes 1179656 | tf_op jit(solution)/shard_map/ppermute | solution.py:38
  151.1 24.9 %collective-permute-start.42 = (bf16[256,4096]{1,0:T(8,128)(2,1)}, bf16[256,4096]{1,0:T(8,128)(2,1)}, u32[]{:S(2)}, u32[]{:S(2)}) collective-permute-start(bf16[256,4096]{1,0:T(8,128)(2,1)} %collective-permute-done.39.refs_9_.refs_4_), channel_id=1, source_target_pairs={{0,4},{4,0},{8,12},{12,8},{16,20},{20,16},{24,28},{28,24},{1,5},{5... | collective-permute-start | bytes 6291464 | tf_op jit(solution)/shard_map/ppermute | solution.py:38
  174.5 37.1 %collective-permute-start.52 = (bf16[3,256,1024]{2,1,0:T(8,128)(2,1)}, bf16[3,256,1024]{2,1,0:T(8,128)(2,1)}, u32[]{:S(2)}, u32[]{:S(2)}) collective-permute-start(bf16[3,256,1024]{2,1,0:T(8,128)(2,1)} %shard_map.108.refs_5_), channel_id=1, source_target_pairs={{0,16},{4,20},{8,24},{12,28},{16,0},{20,4},{24,8},{28,12},{1,17},{... | collective-permute-start | bytes 4718600 | tf_op jit(solution)/shard_map/ppermute | solution.py:38
  176.0 36.8 %collective-permute-start.51 = (bf16[3,256,1024]{2,1,0:T(8,128)(2,1)}, bf16[3,256,1024]{2,1,0:T(8,128)(2,1)}, u32[]{:S(2)}, u32[]{:S(2)}) collective-permute-start(bf16[3,256,1024]{2,1,0:T(8,128)(2,1)} %shard_map.108.refs_5_), channel_id=1, source_target_pairs={{0,8},{4,12},{8,0},{12,4},{16,24},{20,28},{24,16},{28,20},{1,9},{5... | collective-permute-start | bytes 4718600 | tf_op jit(solution)/shard_map/ppermute | solution.py:38
  198.8 20.4 %collective-permute-start.49 = (bf16[512,512]{1,0:T(8,128)(2,1)}, bf16[512,512]{1,0:T(8,128)(2,1)S(1)}, u32[]{:S(2)}, u32[]{:S(2)}) collective-permute-start(bf16[512,512]{1,0:T(8,128)(2,1)} %get-tuple-element.279), channel_id=1, source_target_pairs={{3,2},{0,1},{7,6},{4,5},{11,10},{8,9},{15,14},{12,13},{19,18},{16,... | collective-permute-start | bytes 1572872 | tf_op jit(solution)/shard_map/ppermute | solution.py:118
  220.4 24.4 %collective-permute-start.54 = (bf16[512,512]{1,0:T(8,128)(2,1)S(1)}, bf16[512,512]{1,0:T(8,128)(2,1)S(1)}, u32[]{:S(2)}, u32[]{:S(2)}) collective-permute-start(bf16[512,512]{1,0:T(8,128)(2,1)S(1)} %add_convert_fusion.6), channel_id=1, source_target_pairs={{0,2},{1,3},{2,0},{3,1},{4,6},{5,7},{6,4},{7,5},{8,10},{9,11},{10,... | collective-permute-start | bytes 1572872 | tf_op jit(solution)/shard_map/ppermute | solution.py:38
  222.9 22.0 %collective-permute-start.53 = (bf16[512,512]{1,0:T(8,128)(2,1)S(1)}, bf16[512,512]{1,0:T(8,128)(2,1)S(1)}, u32[]{:S(2)}, u32[]{:S(2)}) collective-permute-start(bf16[512,512]{1,0:T(8,128)(2,1)S(1)} %copy-done.27), channel_id=1, source_target_pairs={{0,1},{1,0},{2,3},{3,2},{4,5},{5,4},{6,7},{7,6},{8,9},{9,8},{10,11... | collective-permute-start | bytes 1572872 | tf_op jit(solution)/shard_map/ppermute | solution.py:38
  225.3 20.9 %collective-permute-start.56 = (bf16[3,128,1024]{2,1,0:T(8,128)(2,1)S(1)}, bf16[3,128,1024]{2,1,0:T(8,128)(2,1)S(1)}, u32[]{:S(2)}, u32[]{:S(2)}) collective-permute-start(bf16[3,128,1024]{2,1,0:T(8,128)(2,1)S(1)} %slice.82), channel_id=1, source_target_pairs={{0,16},{4,20},{8,24},{12,28},{16,0},{20,4},{24,8},{28,12},{1,17},{... | collective-permute-start | bytes 2359304 | tf_op jit(solution)/shard_map/ppermute | solution.py:38
  226.5 19.8 %collective-permute-start.55 = (bf16[3,128,1024]{2,1,0:T(8,128)(2,1)S(1)}, bf16[3,128,1024]{2,1,0:T(8,128)(2,1)S(1)}, u32[]{:S(2)}, u32[]{:S(2)}) collective-permute-start(bf16[3,128,1024]{2,1,0:T(8,128)(2,1)S(1)} %slice.81), channel_id=1, source_target_pairs={{0,8},{4,12},{8,0},{12,4},{16,24},{20,28},{24,16},{28,20},{1,9},{5... | collective-permute-start | bytes 2359304 | tf_op jit(solution)/shard_map/ppermute | solution.py:38
  246.4 24.3 %collective-permute-start.58 = (bf16[512,512]{1,0:T(8,128)(2,1)S(1)}, bf16[512,512]{1,0:T(8,128)(2,1)S(1)}, u32[]{:S(2)}, u32[]{:S(2)}) collective-permute-start(bf16[512,512]{1,0:T(8,128)(2,1)S(1)} %fusion.9.refs_0_), channel_id=1, source_target_pairs={{0,2},{1,3},{2,0},{3,1},{4,6},{5,7},{6,4},{7,5},{8,10},{9,11},{10,... | collective-permute-start | bytes 1572872 | tf_op jit(solution)/shard_map/ppermute | solution.py:38
  248.9 21.9 %collective-permute-start.57 = (bf16[512,512]{1,0:T(8,128)(2,1)S(1)}, bf16[512,512]{1,0:T(8,128)(2,1)S(1)}, u32[]{:S(2)}, u32[]{:S(2)}) collective-permute-start(bf16[512,512]{1,0:T(8,128)(2,1)S(1)} %fusion.9.refs_0_), channel_id=1, source_target_pairs={{0,1},{1,0},{2,3},{3,2},{4,5},{5,4},{6,7},{7,6},{8,9},{9,8},{10,11... | collective-permute-start | bytes 1572872 | tf_op jit(solution)/shard_map/ppermute | solution.py:38
  249.3 22.7 %collective-permute-start.61 = (bf16[3,256,1024]{2,1,0:T(8,128)(2,1)}, bf16[3,256,1024]{2,1,0:T(8,128)(2,1)}, u32[]{:S(2)}, u32[]{:S(2)}) collective-permute-start(bf16[3,256,1024]{2,1,0:T(8,128)(2,1)} %shard_map.108.refs_5_), channel_id=1, source_target_pairs={{0,4},{4,0},{8,12},{12,8},{16,20},{20,16},{24,28},{28,24},{1,5},{5... | collective-permute-start | bytes 4718600 | tf_op jit(solution)/shard_map/ppermute | solution.py:38
  270.8 17.5 %collective-permute-start.62 = (bf16[3,256,1024]{2,1,0:T(8,128)(2,1)}, bf16[3,256,1024]{2,1,0:T(8,128)(2,1)}, u32[]{:S(2)}, u32[]{:S(2)}) collective-permute-start(bf16[3,256,1024]{2,1,0:T(8,128)(2,1)} %collective-permute-done.51.refs_7_), channel_id=1, source_target_pairs={{0,4},{4,0},{8,12},{12,8},{16,20},{20,16},{24,28},{28,24},{1,5},{5... | collective-permute-start | bytes 4718600 | tf_op jit(solution)/shard_map/ppermute | solution.py:38
  270.8 18.2 %collective-permute-start.63 = (bf16[3,256,1024]{2,1,0:T(8,128)(2,1)}, bf16[3,256,1024]{2,1,0:T(8,128)(2,1)}, u32[]{:S(2)}, u32[]{:S(2)}) collective-permute-start(bf16[3,256,1024]{2,1,0:T(8,128)(2,1)} %collective-permute-done.52.refs_9_), channel_id=1, source_target_pairs={{0,4},{4,0},{8,12},{12,8},{16,20},{20,16},{24,28},{28,24},{1,5},{5... | collective-permute-start | bytes 4718600 | tf_op jit(solution)/shard_map/ppermute | solution.py:38
  271.3 17.7 %collective-permute-start.64 = (bf16[3,256,1024]{2,1,0:T(8,128)(2,1)S(1)}, bf16[3,256,1024]{2,1,0:T(8,128)(2,1)}, u32[]{:S(2)}, u32[]{:S(2)}) collective-permute-start(bf16[3,256,1024]{2,1,0:T(8,128)(2,1)S(1)} %constant_dynamic-update-slice_fusion.4.refs_11_), channel_id=1, source_target_pairs={{0,4},{4,0},{8,12},{12,8},{16,20},{20,16},{24,28},{28,24},{1,5},{5... | collective-permute-start | bytes 4718600 | tf_op jit(solution)/shard_map/ppermute | solution.py:38
  318.3 25.3 %collective-permute-start.68 = (bf16[512,512]{1,0:T(8,128)(2,1)S(1)}, bf16[512,512]{1,0:T(8,128)(2,1)S(1)}, u32[]{:S(2)}, u32[]{:S(2)}) collective-permute-start(bf16[512,512]{1,0:T(8,128)(2,1)S(1)} %add_convert_fusion.5), channel_id=1, source_target_pairs={{0,2},{1,3},{2,0},{3,1},{4,6},{5,7},{6,4},{7,5},{8,10},{9,11},{10,... | collective-permute-start | bytes 1572872 | tf_op jit(solution)/shard_map/ppermute | solution.py:38
  321.7 22.1 %collective-permute-start.67 = (bf16[512,512]{1,0:T(8,128)(2,1)S(1)}, bf16[512,512]{1,0:T(8,128)(2,1)S(1)}, u32[]{:S(2)}, u32[]{:S(2)}) collective-permute-start(bf16[512,512]{1,0:T(8,128)(2,1)S(1)} %copy-done.30), channel_id=1, source_target_pairs={{0,1},{1,0},{2,3},{3,2},{4,5},{5,4},{6,7},{7,6},{8,9},{9,8},{10,11... | collective-permute-start | bytes 1572872 | tf_op jit(solution)/shard_map/ppermute | solution.py:38
  348.4 23.3 %collective-permute-start.74 = (bf16[512,512]{1,0:T(8,128)(2,1)}, bf16[512,512]{1,0:T(8,128)(2,1)}, u32[]{:S(2)}, u32[]{:S(2)}) collective-permute-start(bf16[512,512]{1,0:T(8,128)(2,1)} %add_convert_fusion.4), channel_id=1, source_target_pairs={{0,24},{4,28},{8,16},{12,20},{16,8},{20,12},{24,0},{28,4},{1,25},{... | collective-permute-start | bytes 1572872 | tf_op jit(solution)/shard_map/ppermute | solution.py:38
  (39 other events, 523.2 us)
where the time goes:
time: 387 us; the launch traced here: 383 us
  waiting for transfers between devices  206 us (53%)
  starting transfers between devices  72.1 us (19%)
  Pallas kernels  54.6 us (14%)
  local copies, waits for them, and re-layouts  35.3 us (9%)
  other arithmetic  10.8 us (3%)
    ppermute x45, waiting for transfers between devices, swap(): return lax.ppermute(block, axis, [(i, i ^ step) for i in range(size)])  169 us
    ppermute x45, starting transfers between devices, swap(): return lax.ppermute(block, axis, [(i, i ^ step) for i in range(size)])  51.4 us
    ppermute x2, waiting for transfers between devices, gather_cols(): ends = lax.ppermute(passed, 'col', [(2, 3), (1, 0)])  19.5 us
    ppermute x2, waiting for transfers between devices, collect(): early = lax.ppermute(terms[3], 'col', [(3, 2), (0, 1)])  17.5 us
    pallas_call x1, Pallas kernels, retain(): pl.pallas_call(functools.partial(retain_kernel, rows, counts, heads), out...  14.2 us
    ppermute x2, starting transfers between devices, collect(): early = lax.ppermute(terms[3], 'col', [(3, 2), (0, 1)])  14.2 us
    pallas_call x1, Pallas kernels, feed(): pl.pallas_call(functools.partial(feed_kernel, rows, counts, tile), out_sh...  11.7 us
    unnamed x41, local copies, waits for them, and re-layouts  9.99 us
  transfers between devices with their start and end apart: 53, of which 22 were waited for; matrix products, arithmetic and copies ran while one was open for 8% of the time, Pallas kernels for 9%

commit v1 on v0

--- a/solution.py
+++ b/solution.py
@@ -42,29 +42,31 @@
     return lax.optimization_barrier((value,) + earlier)[0]
 
 
-def gather_links(block, arrived=None, halves=(), whole=()):
-    across, along = arrived or (swap(block, "row", 2), swap(block, "row", 4))
-    pieces = {0: block, 2: across, 4: along}
+def gather_links(block, halves=()):
+    across, along = swap(block, "row", 2), swap(block, "row", 4)
+    pieces = {0: (block,), 2: (across,), 4: (along,)}
     axis = block.ndim - 2
     half = block.shape[axis] // 2
     across, along = after((across, along), *halves)
     upper = swap(lax.slice_in_dim(along, 0, half, axis=axis), "row", 2)
     lower = swap(lax.slice_in_dim(across, half, 2 * half, axis=axis), "row", 4)
-    pieces[6] = jnp.concatenate(after((upper, lower), *whole), axis=axis)
+    pieces[6] = (upper, lower)
     return pieces
 
 
-def gather_cores(pieces, earlier=()):
-    own = pieces[0] if earlier else after(pieces[0], pieces[2], pieces[4])
+def gather_cores(pieces, earlier=(), whole=()):
+    if not earlier:
+        pieces[0] = (after(pieces[0][0], pieces[2][0], pieces[4][0]),)
     for j in (0, 2, 4, 6):
-        pieces[j | 1] = swap(after(pieces[j], *earlier) if j else own, "row", 1)
+        wait = (*earlier, *whole) if j == 6 else earlier if j else ()
+        pieces[j | 1] = tuple(swap(after(part, *wait), "row", 1) for part in pieces[j])
     return [pieces[j] for j in range(8)]
 
 
-def gather_rows(block, direct=False, **order):
+def gather_rows(block, direct=False, halves=(), core=(), whole=()):
     size = lax.axis_size("row")
     if size == 8 and not direct:
-        return gather_cores(gather_links(block, **order))
+        return gather_cores(gather_links(block, halves=halves), earlier=core, whole=whole)
     pieces = {0: block}
     if size == 8:
         for j in (2, 4, 6):
@@ -76,11 +78,11 @@
     for bit in bits:
         for j in sorted(pieces):
             pieces[j | bit] = swap(pieces[j], "row", bit)
-    return [pieces[j] for j in range(size)]
+    return [(pieces[j],) for j in range(size)]
 
 
 def last_parts(pieces):
-    return (pieces[6],) if len(pieces) == 8 else (pieces[-1],)
+    return pieces[6] if len(pieces) == 8 else pieces[-1]
 
 
 def mark(block, lengths):
@@ -90,8 +92,10 @@
 
 
 def read_marks(pieces, per_row):
-    rows = pieces[0].shape[0] - 2 * TILE
-    digits = jnp.concatenate([piece[rows : rows + per_row, :2] for piece in pieces], axis=0).astype(jnp.int32)
+    last = [piece[-1] for piece in pieces]
+    digits = jnp.concatenate(
+        [block[block.shape[0] - 2 * TILE :][:per_row, :2] for block in last], axis=0
+    ).astype(jnp.int32)
     return digits[:, 0] * TILE + digits[:, 1]
 
 
@@ -111,17 +115,16 @@
     return [(block,), (near,), (far,), (middle, ends)]
 
 
-def collect(terms, later=()):
+def collect(terms):
     if lax.axis_size("col") != 4:
-        parts = exchange(terms)
-        return parts, parts[1:2]
+        return exchange(terms)
     early = lax.ppermute(terms[3], "col", [(3, 2), (0, 1)])
     middle = lax.ppermute(terms[3], "col", [(1, 2), (2, 1)])
-    term1, term2, early = after((terms[1], terms[2], early), middle, *later)
+    term1, term2, early = after((terms[1], terms[2], early), middle)
     near = swap(term1, "col", 1)
     both = term2.astype(jnp.float32) + early.astype(jnp.float32)
     far = swap(both.astype(jnp.bfloat16), "col", 2)
-    return [terms[0], near, far, middle], (early, middle)
+    return [terms[0], near, far, middle]
 
 
 def added(parts):
@@ -246,8 +249,9 @@
     )(place, lengths)
 
 
-def pick_kernel(rows, per_row, turn, place, table, *refs):
-    pieces, out, sem = refs[:rows], refs[rows], refs[rows + 1]
+def pick_kernel(counts, per_row, turn, place, table, *refs):
+    number = sum(counts)
+    pieces, out, sem = split(refs[:number], counts), refs[number], refs[number + 1]
     row = place[0]
 
     def step(i, carry):
@@ -256,13 +260,15 @@
         owner = request // per_row
         tile = (request - owner * per_row) * TILES + (code - request * TILES)
         piece = lax.bitwise_xor(owner, row)
-        source = pl.ds(pl.multiple_of(tile * TILE, TILE), TILE)
         target = pl.ds(pl.multiple_of(i * TILE, TILE), TILE)
-        for j in range(rows):
-
-            @pl.when(piece == j)
-            def _():
-                pltpu.make_async_copy(pieces[j].at[source, :], out.at[target, :], sem).start()
+        for j, parts in enumerate(pieces):
+            tiles = parts[0].shape[0] // TILE
+            for k, part in enumerate(parts):
+
+                @pl.when((piece == j) & (tile // tiles == k))
+                def _():
+                    source = pl.ds(pl.multiple_of((tile - k * tiles) * TILE, TILE), TILE)
+                    pltpu.make_async_copy(part.at[source, :], out.at[target, :], sem).start()
 
         return carry
 
@@ -270,18 +276,18 @@
     pltpu.make_async_copy(out, out, sem).wait()
 
 
-def pick(place, table, pieces, turn):
-    rows = len(pieces)
-    width = pieces[0].shape[1]
-    return pl.pallas_call(
-        functools.partial(pick_kernel, rows, pieces[0].shape[0] // S, turn),
+def pick(place, table, pieces, turn, per_row):
+    flat, counts = flatten(pieces)
+    width = flat[0].shape[1]
+    return pl.pallas_call(
+        functools.partial(pick_kernel, counts, per_row, turn),
         out_shape=jax.ShapeDtypeStruct((S, width), jnp.bfloat16),
-        in_specs=[SMEM, SMEM] + [ANY] * rows,
+        in_specs=[SMEM, SMEM] + [ANY] * len(flat),
         out_specs=VMEM,
         scratch_shapes=[pltpu.SemaphoreType.DMA],
         compiler_params=params(),
         cost_estimate=cost(0, 4 * S * width),
-    )(place, table, *pieces)
+    )(place, table, *flat)
 
 
 def spread_kernel(rows, per_row, total, place, lengths, bins, starts, *refs):
@@ -317,6 +323,7 @@
 
 
 def spread(place, lengths, bins, starts, pieces, rows, per_row):
+    pieces = [block for (block,) in pieces]
     width = pieces[0].shape[1]
     return pl.pallas_call(
         functools.partial(spread_kernel, rows, per_row, len(pieces)),
@@ -337,6 +344,11 @@
 
 def flatten(parts):
     return [part for entry in parts for part in entry], tuple(len(entry) for entry in parts)
+
+
+def split(refs, counts):
+    refs = list(refs)
+    return [tuple(refs.pop(0) for _ in range(count)) for count in counts]
 
 
 def read_parts(refs, counts):
@@ -353,21 +365,29 @@
     return values * (1.0 / (1.0 + jnp.exp(-values)))
 
 
-def retain_kernel(rows, counts, heads, place, decays, cosine, sine, seg_col, seg_row, *refs):
+def row_parts(weights, axis):
+    for j, parts in enumerate(weights):
+        size = parts[0].shape[axis]
+        for k, part in enumerate(parts):
+            yield j, part, k * size, size
+
+
+def retain_kernel(weight_counts, counts, heads, place, decays, cosine, sine, seg_col, seg_row, *refs):
     cols, number = len(counts), sum(counts)
-    tokens, weights = refs[:number], refs[number : number + rows]
-    mixed, normed, gathered, sems = refs[number + rows :]
+    rows, total_weights = len(weight_counts), sum(weight_counts)
+    tokens, weights = refs[:number], split(refs[number : number + total_weights], weight_counts)
+    mixed, normed, gathered, sems = refs[number + total_weights :]
     depth = D // rows
     width = D // cols
     parts = ((0, 2 * KEY), (2 * KEY, VAL), (2 * KEY + VAL, VAL))
 
     for head in range(heads):
-        for i, (low, size) in enumerate(parts):
-            columns = pl.ds(head * HEAD_WIDTH + low, size)
-            for j in range(rows):
-                where = pl.ds(pl.multiple_of(lax.bitwise_xor(place[0], j) * depth, depth), depth)
+        for i, (low, span) in enumerate(parts):
+            columns = pl.ds(head * HEAD_WIDTH + low, span)
+            for j, part, start, size in row_parts(weights, 0):
+                where = pl.ds(pl.multiple_of(lax.bitwise_xor(place[0], j) * depth + start, size), size)
                 pltpu.make_async_copy(
-                    weights[j].at[:, columns], gathered.at[where, columns], sems.at[head * 3 + i]
+                    part.at[:, columns], gathered.at[where, columns], sems.at[head * 3 + i]
                 ).start()
 
     total = jnp.zeros((S, 1), jnp.float32)
@@ -415,10 +435,11 @@
     rows, cols = len(weights), len(tokens)
     heads = HEADS // cols
     flat, counts = flatten(tokens)
-    return pl.pallas_call(
-        functools.partial(retain_kernel, rows, counts, heads),
+    flat_weights, weight_counts = flatten(weights)
+    return pl.pallas_call(
+        functools.partial(retain_kernel, weight_counts, counts, heads),
         out_shape=jax.ShapeDtypeStruct((S, heads * VAL), jnp.bfloat16),
-        in_specs=[SMEM, SMEM] + [VMEM] * (4 + len(flat)) + [ANY] * rows,
+        in_specs=[SMEM, SMEM] + [VMEM] * (4 + len(flat)) + [ANY] * len(flat_weights),
         out_specs=VMEM,
         scratch_shapes=[
             pltpu.VMEM((S, D), jnp.bfloat16),
@@ -427,16 +448,16 @@
         ],
         compiler_params=params(),
         cost_estimate=cost(2 * S * D * HEAD_WIDTH * heads * 1.3, 2 * D * HEAD_WIDTH * heads),
-    )(place, decays, cosine, sine, seg_col, seg_row, *flat, *weights)
+    )(place, decays, cosine, sine, seg_col, seg_row, *flat, *flat_weights)
 
 
 def load_terms(rows, cols, place, views, gathered, sem):
     ratio = rows // cols
-    for j in range(rows):
+    for j, view, start, size in views:
         owner = lax.bitwise_xor(place[0], j)
         target = owner // ratio
         slot = lax.bitwise_xor(target, place[1]) * ratio + (owner - target * ratio)
-        pltpu.make_async_copy(views[j], gathered.at[slot], sem).start()
+        pltpu.make_async_copy(view, gathered.at[slot, pl.ds(start, size), :], sem).start()
 
 
 def put_terms(rows, cols, left, gathered, sem, outs):
@@ -448,11 +469,15 @@
         outs[k][:, i * depth : (i + 1) * depth] = DOT_T(left, gathered[slot]).astype(jnp.bfloat16)
 
 
-def mix_kernel(rows, cols, place, mixed, *refs):
-    weights, outs = refs[:rows], refs[rows : rows + cols]
-    gathered, sem = refs[rows + cols :]
+def mix_kernel(weight_counts, cols, place, mixed, *refs):
+    rows, number = len(weight_counts), sum(weight_counts)
+    weights, outs = split(refs[:number], weight_counts), refs[number : number + cols]
+    gathered, sem = refs[number + cols :]
     units = mixed.shape[1]
-    views = [ref.at[:, pl.ds(ref.shape[1] - units, units)] for ref in weights]
+    views = [
+        (j, part.at[:, pl.ds(part.shape[1] - units, units)], start, size)
+        for j, part, start, size in row_parts(weights, 0)
+    ]
     load_terms(rows, cols, place, views, gathered, sem)
     put_terms(rows, cols, mixed[...], gathered, sem, outs)
 
@@ -460,10 +485,11 @@
 def mix(place, mixed, weights, cols):
     rows = len(weights)
     width = D // cols
-    return pl.pallas_call(
-        functools.partial(mix_kernel, rows, cols),
+    flat, weight_counts = flatten(weights)
+    return pl.pallas_call(
+        functools.partial(mix_kernel, weight_counts, cols),
         out_shape=[jax.ShapeDtypeStruct((S, width), jnp.bfloat16)] * cols,
-        in_specs=[SMEM, VMEM] + [ANY] * rows,
+        in_specs=[SMEM, VMEM] + [ANY] * len(flat),
         out_specs=[VMEM] * cols,
         scratch_shapes=[
             pltpu.VMEM((rows, D // rows, mixed.shape[1]), jnp.bfloat16),
@@ -471,27 +497,29 @@
         ],
         compiler_params=params(),
         cost_estimate=cost(2 * S * D * mixed.shape[1], 2 * D * mixed.shape[1]),
-    )(place, mixed, *weights)
-
-
-def feed_kernel(rows, counts, tile, place, *refs):
+    )(place, mixed, *flat)
+
+
+def feed_kernel(weight_counts, counts, tile, place, *refs):
     cols, number = len(counts), sum(counts)
+    rows, last = len(weight_counts), sum(counts) + sum(weight_counts)
     tokens = refs[:number]
-    weights = refs[number : number + rows]
-    outs = refs[number + rows : number + rows + cols]
-    ordered, hidden, gathered, gathered_down, sems, sem_down = refs[number + rows + cols :]
+    weights = split(refs[number:last], weight_counts)
+    outs = refs[last : last + cols]
+    ordered, hidden, gathered, gathered_down, sems, sem_down = refs[last + cols :]
     depth = D // rows
     width = D // cols
     steps = gathered.shape[2] // tile
 
     for step in range(steps):
         columns = pl.ds(step * tile, tile)
-        for j in range(rows):
-            where = pl.ds(pl.multiple_of(lax.bitwise_xor(place[0], j) * depth, depth), depth)
+        for j, part, start, size in row_parts(weights, 1):
+            where = pl.ds(pl.multiple_of(lax.bitwise_xor(place[0], j) * depth + start, size), size)
             pltpu.make_async_copy(
-                weights[j].at[pl.ds(1, 2), :, columns], gathered.at[:, where, columns], sems.at[step]
+                part.at[pl.ds(1, 2), :, columns], gathered.at[:, where, columns], sems.at[step]
             ).start()
-    load_terms(rows, cols, place, [ref.at[0] for ref in weights], gathered_down, sem_down)
+    views = [(j, part.at[0], start, size) for j, part, start, size in row_parts(weights, 1)]
+    load_terms(rows, cols, place, views, gathered_down, sem_down)
 
     total = jnp.zeros((S, 1), jnp.float32)
     for k, block in enumerate(read_parts(tokens, counts)):
@@ -513,13 +541,14 @@
 
 def feed(place, tokens, weights):
     rows, cols = len(weights), len(tokens)
-    units = weights[0].shape[2]
+    units = weights[0][0].shape[2]
     tile = min(units, 512)
     flat, counts = flatten(tokens)
-    return pl.pallas_call(
-        functools.partial(feed_kernel, rows, counts, tile),
+    flat_weights, weight_counts = flatten(weights)
+    return pl.pallas_call(
+        functools.partial(feed_kernel, weight_counts, counts, tile),
         out_shape=[jax.ShapeDtypeStruct((S, D // cols), jnp.bfloat16)] * cols,
-        in_specs=[SMEM] + [VMEM] * len(flat) + [ANY] * rows,
+        in_specs=[SMEM] + [VMEM] * len(flat) + [ANY] * len(flat_weights),
         out_specs=[VMEM] * cols,
         scratch_shapes=[
             pltpu.VMEM((S, D), jnp.bfloat16),
@@ -531,7 +560,7 @@
         ],
         compiler_params=params(),
         cost_estimate=cost(6 * S * D * units, 6 * D * units),
-    )(place, *flat, *weights)
+    )(place, *flat, *flat_weights)
 
 
 def shards(hidden_states, lengths, qkvg_master, gateup_master, out_master, down_master):
@@ -563,7 +592,7 @@
         seg = jnp.broadcast_to(segments[:, None], (TILES, TILE)).reshape(S)
         positions = ((jnp.maximum(codes, 0) % TILES)[:, None] * TILE + jnp.arange(TILE)[None, :]).reshape(S)
         angle = positions.astype(jnp.float32)[:, None] * freq[None, :]
-        own = pick(place, table, everyone, turn)
+        own = pick(place, table, everyone, turn, per_row)
         return own, (jnp.cos(angle), jnp.sin(angle), seg[:, None], seg[None, :])
 
     own, tables = begin(0)
@@ -572,30 +601,26 @@
     rest = [part for entry in tokens[3:] for part in entry]
     feed_parts = exchange(list(after(tuple(feed_cut), *rest)))
     front_pieces = gather_rows(
-        after(front_blocks, *last_parts(everyone)), halves=ahead, whole=(*rest, *tables, *feed_parts[1:])
+        after(front_blocks, *last_parts(everyone)), halves=ahead, core=rest, whole=(*tables, feed_cut[0])
     )
 
     mixed = retain(place, decays, *tables, tokens, front_pieces)
     terms = mix(place, mixed, front_pieces, cols)
-    feed_blocks = after(join(feed_parts, place), *last_parts(front_pieces))
-    whole = rows == 8
-    arrived = (swap(feed_blocks, "row", 2), swap(feed_blocks, "row", 4)) if whole else ()
-    attended, early = collect(terms, later=arrived)
+    feed_blocks = join(list(after(tuple(feed_parts), terms[0])), place)
+    attended = collect(list(after(tuple(terms), feed_blocks)))
     residual = own.astype(jnp.float32) + added(attended)
-    sent = residual.astype(jnp.bfloat16)
-    if whole:
-        links = gather_links(feed_blocks, arrived=arrived, halves=early)
-        mid_tokens = gather_cols(after(sent, links[6]))
-        feed_pieces = gather_cores(links, earlier=(mid_tokens[1][0], mid_tokens[2][0]))
+    mid_tokens = gather_cols(residual.astype(jnp.bfloat16))
+    if rows == 8:
+        links = gather_links(feed_blocks, halves=attended[1:])
+        feed_pieces = gather_cores(links, earlier=links[6], whole=mid_tokens[3][:1])
     else:
-        mid_tokens = gather_cols(sent)
         feed_pieces = gather_rows(feed_blocks)
 
     weights = (front_blocks[:, :width], feed_blocks[1:], front_blocks[:, width:].T, feed_blocks[0].T)
     weights = lax.optimization_barrier(weights)
 
     def rest_of_layer(residual, tokens, feed_pieces):
-        fed, _ = collect(feed(place, tokens, feed_pieces))
+        fed = collect(feed(place, tokens, feed_pieces))
         return gather_rows((residual + added(fed)).astype(jnp.bfloat16), direct=True)
 
     first = rest_of_layer(residual, mid_tokens, [after(feed_pieces[0], *weights)] + feed_pieces[1:])
@@ -607,7 +632,7 @@
         for turn in range(1, per_row):
             own, tables = begin(turn)
             mixed = retain(place, decays, *tables, gather_cols(own), front_pieces)
-            attended, _ = collect(mix(place, mixed, front_pieces, cols))
+            attended = collect(mix(place, mixed, front_pieces, cols))
             residual = own.astype(jnp.float32) + added(attended)
             pieces = pieces + rest_of_layer(residual, gather_cols(residual.astype(jnp.bfloat16)), feed_pieces)
         return finish(pieces)

time: 387 us -> 399 us (1.031)
  waiting for transfers between devices: 206 us -> 229 us
  local copies, waits for them, and re-layouts: 35.3 us -> 28.8 us
    ppermute x2, waiting for transfers between devices: 19.5 us -> 37.8 us  [gather_cols(): ends = lax.ppermute(passed, 'col', [(2, 3), (1, 0)])]
    unnamed x41 -> x74, local copies, waits for them, and re-layouts: 9.99 us -> 11.9 us
    ppermute x45 -> x48, waiting for transfers between devices: 169 us -> 170 us  [swap(): return lax.ppermute(block, axis, [(i, i ^ step) for i in range(size)])]
    ppermute x45 -> x48, starting transfers between devices: 51.4 us -> 52.1 us  [swap(): return lax.ppermute(block, axis, [(i, i ^ step) for i in range(size)])]
  transfers between devices with their start and end apart: 53 -> 56, of which waited for: 22 -> 25; matrix products, arithmetic and copies ran while one was open for 8% -> 6% of each run, Pallas kernels for 9% -> 8%
where the time goes in v1:
time: 399 us; the launch traced here: 396 us
  waiting for transfers between devices  229 us (57%)
  starting transfers between devices  74.2 us (19%)
  Pallas kernels  53.2 us (13%)
  local copies, waits for them, and re-layouts  28.8 us (7%)
  other arithmetic  7.59 us (2%)
    ppermute x48, waiting for transfers between devices, swap(): return lax.ppermute(block, axis, [(i, i ^ step) for i in range(size)])  170 us
    ppermute x48, starting transfers between devices, swap(): return lax.ppermute(block, axis, [(i, i ^ step) for i in range(size)])  52.1 us
    ppermute x2, waiting for transfers between devices, gather_cols(): ends = lax.ppermute(passed, 'col', [(2, 3), (1, 0)])  37.8 us
    ppermute x2, waiting for transfers between devices, collect(): early = lax.ppermute(terms[3], 'col', [(3, 2), (0, 1)])  20.8 us
    ppermute x2, starting transfers between devices, collect(): early = lax.ppermute(terms[3], 'col', [(3, 2), (0, 1)])  15.5 us
    pallas_call x1, Pallas kernels, retain(): pl.pallas_call(functools.partial(retain_kernel, weight_counts, counts, he...  14.2 us
    unnamed x74, local copies, waits for them, and re-layouts  11.9 us
    pallas_call x1, Pallas kernels, feed(): pl.pallas_call(functools.partial(feed_kernel, weight_counts, counts, tile...  11.7 us
  transfers between devices with their start and end apart: 56, of which 25 were waited for; matrix products, arithmetic and copies ran while one was open for 6% of the time, Pallas kernels for 8%

profile of v1, /device:TPU:0, one launch (start us, length us, event | category | flops | bytes accessed | tf_op | source)
XLA Modules:
  0.0 395.9 jit_solution(8152266908595443982)
XLA Ops:
  3.0 3.7 shard_map.101
  6.7 3.0 collective-permute-start.24
  15.3 18.2 %collective-permute-done.24.refs_4_ = bf16[1056,512]{1,0:T(8,128)(2,1)S(1)} collective-permute-done((bf16[1056,512]{1,0:T(8,128)(2,1)S(1)}, bf16[1056,512]{1,0:T(8,128)(2,1)S(1)}, u32[]{:S(2)}, u32[]{:S(2)}) %collective-permute-start.24) | collective-permute-done | bytes 1081376 | tf_op jit(solution)/shard_map/ppermute | solution.py:38
  42.9 6.9 %collective-permute-done.30.refs_7_ = bf16[528,512]{1,0:T(8,128)(2,1)S(1)} collective-permute-done((bf16[528,512]{1,0:T(8,128)(2,1)S(1)}, bf16[528,512]{1,0:T(8,128)(2,1)S(1)}, u32[]{:S(2)}, u32[]{:S(2)}) %collective-permute-start.30) | collective-permute-done | bytes 540704 | tf_op jit(solution)/shard_map/ppermute | solution.py:38
  49.8 3.3 collective-permute-done.38.refs_3_
  64.9 4.2 %shard_map.102 = (s32[64]{0:T(128)S(1)}, s32[16]{0:T(128)S(1)}, s32[16]{0:T(128)S(1)}, s32[1]{0:T(128)}) custom-call(s32[2]{0:T(128)S(1)} %pad_add_fusion.place, s32[16]{0:T(128)} %add_bitcast_fusion.lengths), custom_call_target="tpu_custom_call" | custom-call | tf_op jit(solution)/shard_map/pallas_call | solution.py:242
  69.1 3.6 shard_map.103.refs_0_
  72.7 11.9 %collective-permute-start.35 = (bf16[512,512]{1,0:T(8,128)(2,1)}, bf16[512,512]{1,0:T(8,128)(2,1)S(1)}, u32[]{:S(2)}, u32[]{:S(2)}) collective-permute-start(bf16[512,512]{1,0:T(8,128)(2,1)} %shard_map.103.refs_0_), channel_id=1, source_target_pairs={{0,2},{1,3},{2,0},{3,1},{4,6},{5,7},{6,4},{7,5},{8,10},{9,11},{10,... | collective-permute-start | bytes 1572872 | tf_op jit(solution)/shard_map/ppermute | solution.py:38
  84.7 24.2 %collective-permute-done.35.refs_2_ = bf16[512,512]{1,0:T(8,128)(2,1)S(1)} collective-permute-done((bf16[512,512]{1,0:T(8,128)(2,1)}, bf16[512,512]{1,0:T(8,128)(2,1)S(1)}, u32[]{:S(2)}, u32[]{:S(2)}) %collective-permute-start.35) | collective-permute-done | bytes 524320 | tf_op jit(solution)/shard_map/ppermute | solution.py:38
  111.4 14.6 %collective-permute-done.37.refs_4_ = bf16[512,512]{1,0:T(8,128)(2,1)S(1)} collective-permute-done((bf16[512,512]{1,0:T(8,128)(2,1)S(1)}, bf16[512,512]{1,0:T(8,128)(2,1)S(1)}, u32[]{:S(2)}, u32[]{:S(2)}) %collective-permute-start.37) | collective-permute-done | bytes 524320 | tf_op jit(solution)/shard_map/ppermute | solution.py:114
  133.7 3.2 shard_map.105
  139.7 13.7 %collective-permute-done.45.refs_12_.refs_7_ = bf16[128,4096]{1,0:T(8,128)(2,1)} collective-permute-done((bf16[128,4096]{1,0:T(8,128)(2,1)}, bf16[128,4096]{1,0:T(8,128)(2,1)}, u32[]{:S(2)}, u32[]{:S(2)}) %collective-permute-start.45) | collective-permute-done | bytes 1048608 | tf_op jit(solution)/shard_map/ppermute | solution.py:38
  153.5 5.2 %collective-permute-done.44.refs_11_.refs_6_ = bf16[128,4096]{1,0:T(8,128)(2,1)} collective-permute-done((bf16[128,4096]{1,0:T(8,128)(2,1)}, bf16[128,4096]{1,0:T(8,128)(2,1)}, u32[]{:S(2)}, u32[]{:S(2)}) %collective-permute-start.44) | collective-permute-done | bytes 1048608 | tf_op jit(solution)/shard_map/ppermute | solution.py:38
  163.9 14.2 %shard_map.106.mixed = bf16[512,1024]{1,0:T(8,128)(2,1)} custom-call(s32[2]{0:T(128)S(1)} %pad_add_fusion.place, f32[2]{0:T(128)S(1)} %negate_log-plus-one_fusion.decays, f32[512,128]{1,0:T(8,128)} %get-tuple-element.354.cosine, f32[512,128]{1,0:T(8,128)} %get-tuple-element.353.sine, s32[512,1]{1,0:T(8,128)} %copy.32.seg_col, ...), custom_call_target="tpu_custom_call" | custom-call | flops 8375186432 | bytes 12582912 | tf_op jit(solution)/shard_map/pallas_call | solution.py:439
  178.1 6.5 %shard_map.107 = (bf16[512,512]{1,0:T(8,128)(2,1)}, bf16[512,512]{1,0:T(8,128)(2,1)}, bf16[512,512]{1,0:T(8,128)(2,1)}, bf16[512,512]{1,0:T(8,128)(2,1)}) custom-call(s32[2]{0:T(128)S(1)} %pad_add_fusion.place, bf16[512,1024]{1,0:T(8,128)(2,1)} %shard_map.106.mixed, bf16[256,4096]{1,0:T(8,128)(2,1)S(1)} %shard_map.104.refs_5_.refs_0_, ...), custom_call_target="tpu_custom_call" | custom-call | flops 2147483648 | bytes 4194304 | tf_op jit(solution)/shard_map/pallas_call | solution.py:489
  184.7 5.5 %collective-permute-done.49.refs_2_ = bf16[3,64,1024]{2,1,0:T(8,128)(2,1)S(1)} collective-permute-done((bf16[3,64,1024]{2,1,0:T(8,128)(2,1)}, bf16[3,64,1024]{2,1,0:T(8,128)(2,1)S(1)}, u32[]{:S(2)}, u32[]{:S(2)}) %collective-permute-start.49) | collective-permute-done | bytes 393248 | tf_op jit(solution)/shard_map/ppermute | solution.py:38
  194.7 12.6 %collective-permute-start.51 = (bf16[512,512]{1,0:T(8,128)(2,1)S(1)}, bf16[512,512]{1,0:T(8,128)(2,1)S(1)}, u32[]{:S(2)}, u32[]{:S(2)}) collective-permute-start(bf16[512,512]{1,0:T(8,128)(2,1)S(1)} %copy-done.50), channel_id=1, source_target_pairs={{3,2},{0,1},{7,6},{4,5},{11,10},{8,9},{15,14},{12,13},{19,18},{16,... | collective-permute-start | bytes 1572872 | tf_op jit(solution)/shard_map/ppermute | solution.py:121
  207.3 10.0 %collective-permute-done.51 = bf16[512,512]{1,0:T(8,128)(2,1)S(1)} collective-permute-done((bf16[512,512]{1,0:T(8,128)(2,1)S(1)}, bf16[512,512]{1,0:T(8,128)(2,1)S(1)}, u32[]{:S(2)}, u32[]{:S(2)}) %collective-permute-start.51) | collective-permute-done | bytes 524320 | tf_op jit(solution)/shard_map/ppermute | solution.py:121
  217.4 3.3 collective-permute-start.54
  220.7 21.4 %collective-permute-done.54 = bf16[512,512]{1,0:T(8,128)(2,1)S(1)} collective-permute-done((bf16[512,512]{1,0:T(8,128)(2,1)S(1)}, bf16[512,512]{1,0:T(8,128)(2,1)S(1)}, u32[]{:S(2)}, u32[]{:S(2)}) %collective-permute-start.54) | collective-permute-done | bytes 524320 | tf_op jit(solution)/shard_map/ppermute | solution.py:38
  248.6 11.9 %collective-permute-done.63.refs_12_ = bf16[3,128,1024]{2,1,0:T(8,128)(2,1)S(1)} collective-permute-done((bf16[3,128,1024]{2,1,0:T(8,128)(2,1)S(1)}, bf16[3,128,1024]{2,1,0:T(8,128)(2,1)S(1)}, u32[]{:S(2)}, u32[]{:S(2)}) %collective-permute-start.63) | collective-permute-done | bytes 786464 | tf_op jit(solution)/shard_map/ppermute | solution.py:38
  261.1 10.8 %collective-permute-done.56.refs_2_ = bf16[512,512]{1,0:T(8,128)(2,1)S(1)} collective-permute-done((bf16[512,512]{1,0:T(8,128)(2,1)S(1)}, bf16[512,512]{1,0:T(8,128)(2,1)S(1)}, u32[]{:S(2)}, u32[]{:S(2)}) %collective-permute-start.56) | collective-permute-done | bytes 524320 | tf_op jit(solution)/shard_map/ppermute | solution.py:38
  279.6 23.2 %collective-permute-done.58.refs_4_ = bf16[512,512]{1,0:T(8,128)(2,1)S(1)} collective-permute-done((bf16[512,512]{1,0:T(8,128)(2,1)S(1)}, bf16[512,512]{1,0:T(8,128)(2,1)S(1)}, u32[]{:S(2)}, u32[]{:S(2)}) %collective-permute-start.58) | collective-permute-done | bytes 524320 | tf_op jit(solution)/shard_map/ppermute | solution.py:114
  305.3 11.7 %shard_map.109 = (bf16[512,512]{1,0:T(8,128)(2,1)}, bf16[512,512]{1,0:T(8,128)(2,1)}, bf16[512,512]{1,0:T(8,128)(2,1)}, bf16[512,512]{1,0:T(8,128)(2,1)}) custom-call(s32[2]{0:T(128)S(1)} %pad_add_fusion.place, bf16[512,512]{1,0:T(8,128)(2,1)} %copy-done.25, bf16[512,512]{1,0:T(8,128)(2,1)} %copy-done.46, bf16[512,512]{1,0:T(8,128)(2,1)} %copy-done.45, ...), custom_call_target="tpu_custom_call" | custom-call | flops 6442450944 | bytes 12582912 | tf_op jit(solution)/shard_map/pallas_call | solution.py:548
  317.9 3.0 collective-permute-start.68
  320.9 10.8 %collective-permute-done.68 = bf16[512,512]{1,0:T(8,128)(2,1)S(1)} collective-permute-done((bf16[512,512]{1,0:T(8,128)(2,1)}, bf16[512,512]{1,0:T(8,128)(2,1)S(1)}, u32[]{:S(2)}, u32[]{:S(2)}) %collective-permute-start.68) | collective-permute-done | bytes 524320 | tf_op jit(solution)/shard_map/ppermute | solution.py:121
  332.9 3.6 collective-permute-start.71
  336.5 21.7 %collective-permute-done.71 = bf16[512,512]{1,0:T(8,128)(2,1)S(1)} collective-permute-done((bf16[512,512]{1,0:T(8,128)(2,1)S(1)}, bf16[512,512]{1,0:T(8,128)(2,1)S(1)}, u32[]{:S(2)}, u32[]{:S(2)}) %collective-permute-start.71) | collective-permute-done | bytes 524320 | tf_op jit(solution)/shard_map/ppermute | solution.py:38
  360.6 2.9 collective-permute-start.77
  363.4 10.8 %collective-permute-done.73 = bf16[512,512]{1,0:T(8,128)(2,1)} collective-permute-done((bf16[512,512]{1,0:T(8,128)(2,1)}, bf16[512,512]{1,0:T(8,128)(2,1)}, u32[]{:S(2)}, u32[]{:S(2)}) %collective-permute-start.73) | collective-permute-done | bytes 524320 | tf_op jit(solution)/shard_map/ppermute | solution.py:38
  375.7 9.4 %collective-permute-done.77 = bf16[512,512]{1,0:T(8,128)(2,1)} collective-permute-done((bf16[512,512]{1,0:T(8,128)(2,1)}, bf16[512,512]{1,0:T(8,128)(2,1)}, u32[]{:S(2)}, u32[]{:S(2)}) %collective-permute-start.77) | collective-permute-done | bytes 524320 | tf_op jit(solution)/shard_map/ppermute | solution.py:38
  390.5 3.9 conditional.1
  (215 shorter events, 83.6 us)
Async XLA Ops:
  6.7 26.8 %collective-permute-start.24 = (bf16[1056,512]{1,0:T(8,128)(2,1)S(1)}, bf16[1056,512]{1,0:T(8,128)(2,1)S(1)}, u32[]{:S(2)}, u32[]{:S(2)}) collective-permute-start(bf16[1056,512]{1,0:T(8,128)(2,1)S(1)} %pad_maximum_fusion.refs_0_), channel_id=1, source_target_pairs={{0,16},{4,20},{8,24},{12,28},{16,0},{20,4},{24,8},{28,12},{1,17},{... | collective-permute-start | bytes 3244040 | tf_op jit(solution)/shard_map/ppermute | solution.py:38
  9.6 28.3 %collective-permute-start.23 = (bf16[1056,512]{1,0:T(8,128)(2,1)S(1)}, bf16[1056,512]{1,0:T(8,128)(2,1)}, u32[]{:S(2)}, u32[]{:S(2)}) collective-permute-start(bf16[1056,512]{1,0:T(8,128)(2,1)S(1)} %pad_maximum_fusion.refs_0_), channel_id=1, source_target_pairs={{0,8},{4,12},{8,0},{12,4},{16,24},{20,28},{24,16},{28,20},{1,9},{5... | collective-permute-start | bytes 3244040 | tf_op jit(solution)/shard_map/ppermute | solution.py:38
  11.1 24.4 %collective-permute-start.28 = (bf16[64,4096]{1,0:T(8,128)(2,1)}, bf16[64,4096]{1,0:T(8,128)(2,1)S(1)}, u32[]{:S(2)}, u32[]{:S(2)}) collective-permute-start(bf16[64,4096]{1,0:T(8,128)(2,1)} %get-tuple-element.272), channel_id=1, source_target_pairs={{0,1},{1,0},{2,3},{3,2},{4,5},{5,4},{6,7},{7,6},{8,9},{9,8},{10,11... | collective-permute-start | bytes 1572872 | tf_op jit(solution)/shard_map/ppermute | solution.py:38
  12.7 25.2 %collective-permute-start.29 = (bf16[64,4096]{1,0:T(8,128)(2,1)}, bf16[64,4096]{1,0:T(8,128)(2,1)S(1)}, u32[]{:S(2)}, u32[]{:S(2)}) collective-permute-start(bf16[64,4096]{1,0:T(8,128)(2,1)} %get-tuple-element.273), channel_id=1, source_target_pairs={{0,2},{1,3},{2,0},{3,1},{4,6},{5,7},{6,4},{7,5},{8,10},{9,11},{10,... | collective-permute-start | bytes 1572872 | tf_op jit(solution)/shard_map/ppermute | solution.py:38
  33.5 22.6 %collective-permute-start.27 = (bf16[1056,512]{1,0:T(8,128)(2,1)S(1)}, bf16[1056,512]{1,0:T(8,128)(2,1)S(1)}, u32[]{:S(2)}, u32[]{:S(2)}) collective-permute-start(bf16[1056,512]{1,0:T(8,128)(2,1)S(1)} %collective-permute-done.24.refs_4_), channel_id=1, source_target_pairs={{0,4},{4,0},{8,12},{12,8},{16,20},{20,16},{24,28},{28,24},{1,5},{5... | collective-permute-start | bytes 3244040 | tf_op jit(solution)/shard_map/ppermute | solution.py:38
  55.5 70.4 %collective-permute-start.42 = (bf16[256,4096]{1,0:T(8,128)(2,1)S(1)}, bf16[256,4096]{1,0:T(8,128)(2,1)}, u32[]{:S(2)}, u32[]{:S(2)}) collective-permute-start(bf16[256,4096]{1,0:T(8,128)(2,1)S(1)} %shard_map.104.refs_5_.refs_0_), channel_id=1, source_target_pairs={{0,16},{4,20},{8,24},{12,28},{16,0},{20,4},{24,8},{28,12},{1,17},{... | collective-permute-start | bytes 6291464 | tf_op jit(solution)/shard_map/ppermute | solution.py:38
  57.2 69.6 %collective-permute-start.40 = (bf16[256,4096]{1,0:T(8,128)(2,1)S(1)}, bf16[256,4096]{1,0:T(8,128)(2,1)}, u32[]{:S(2)}, u32[]{:S(2)}) collective-permute-start(bf16[256,4096]{1,0:T(8,128)(2,1)S(1)} %shard_map.104.refs_5_.refs_0_), channel_id=1, source_target_pairs={{0,8},{4,12},{8,0},{12,4},{16,24},{20,28},{24,16},{28,20},{1,9},{5... | collective-permute-start | bytes 6291464 | tf_op jit(solution)/shard_map/ppermute | solution.py:38
  72.7 36.2 %collective-permute-start.35 = (bf16[512,512]{1,0:T(8,128)(2,1)}, bf16[512,512]{1,0:T(8,128)(2,1)S(1)}, u32[]{:S(2)}, u32[]{:S(2)}) collective-permute-start(bf16[512,512]{1,0:T(8,128)(2,1)} %shard_map.103.refs_0_), channel_id=1, source_target_pairs={{0,2},{1,3},{2,0},{3,1},{4,6},{5,7},{6,4},{7,5},{8,10},{9,11},{10,... | collective-permute-start | bytes 1572872 | tf_op jit(solution)/shard_map/ppermute | solution.py:38
  84.7 24.4 %collective-permute-start.34 = (bf16[512,512]{1,0:T(8,128)(2,1)}, bf16[512,512]{1,0:T(8,128)(2,1)S(1)}, u32[]{:S(2)}, u32[]{:S(2)}) collective-permute-start(bf16[512,512]{1,0:T(8,128)(2,1)} %shard_map.103.refs_0_), channel_id=1, source_target_pairs={{0,1},{1,0},{2,3},{3,2},{4,5},{5,4},{6,7},{7,6},{8,9},{9,8},{10,11... | collective-permute-start | bytes 1572872 | tf_op jit(solution)/shard_map/ppermute | solution.py:38
  111.3 48.3 %collective-permute-start.39 = (bf16[256,4096]{1,0:T(8,128)(2,1)S(1)}, bf16[256,4096]{1,0:T(8,128)(2,1)}, u32[]{:S(2)}, u32[]{:S(2)}) collective-permute-start(bf16[256,4096]{1,0:T(8,128)(2,1)S(1)} %shard_map.104.refs_5_.refs_0_), channel_id=1, source_target_pairs={{0,4},{4,0},{8,12},{12,8},{16,20},{20,16},{24,28},{28,24},{1,5},{5... | collective-permute-start | bytes 6291464 | tf_op jit(solution)/shard_map/ppermute | solution.py:38
  129.0 24.4 %collective-permute-start.45 = (bf16[128,4096]{1,0:T(8,128)(2,1)}, bf16[128,4096]{1,0:T(8,128)(2,1)}, u32[]{:S(2)}, u32[]{:S(2)}) collective-permute-start(bf16[128,4096]{1,0:T(8,128)(2,1)} %slice.96), channel_id=1, source_target_pairs={{0,16},{4,20},{8,24},{12,28},{16,0},{20,4},{24,8},{28,12},{1,17},{... | collective-permute-start | bytes 3145736 | tf_op jit(solution)/shard_map/ppermute | solution.py:38
  130.5 29.8 %collective-permute-start.43 = (bf16[256,4096]{1,0:T(8,128)(2,1)}, bf16[256,4096]{1,0:T(8,128)(2,1)}, u32[]{:S(2)}, u32[]{:S(2)}) collective-permute-start(bf16[256,4096]{1,0:T(8,128)(2,1)} %collective-permute-done.42.refs_9_.refs_4_), channel_id=1, source_target_pairs={{0,4},{4,0},{8,12},{12,8},{16,20},{20,16},{24,28},{28,24},{1,5},{5... | collective-permute-start | bytes 6291464 | tf_op jit(solution)/shard_map/ppermute | solution.py:38
  132.8 29.8 %collective-permute-start.41 = (bf16[256,4096]{1,0:T(8,128)(2,1)}, bf16[256,4096]{1,0:T(8,128)(2,1)}, u32[]{:S(2)}, u32[]{:S(2)}) collective-permute-start(bf16[256,4096]{1,0:T(8,128)(2,1)} %collective-permute-done.40.refs_7_.refs_2_), channel_id=1, source_target_pairs={{0,4},{4,0},{8,12},{12,8},{16,20},{20,16},{24,28},{28,24},{1,5},{5... | collective-permute-start | bytes 6291464 | tf_op jit(solution)/shard_map/ppermute | solution.py:38
  133.3 25.4 %collective-permute-start.44 = (bf16[128,4096]{1,0:T(8,128)(2,1)}, bf16[128,4096]{1,0:T(8,128)(2,1)}, u32[]{:S(2)}, u32[]{:S(2)}) collective-permute-start(bf16[128,4096]{1,0:T(8,128)(2,1)} %slice.95), channel_id=1, source_target_pairs={{0,8},{4,12},{8,0},{12,4},{16,24},{20,28},{24,16},{28,20},{1,9},{5... | collective-permute-start | bytes 3145736 | tf_op jit(solution)/shard_map/ppermute | solution.py:38
  159.5 25.1 %collective-permute-start.48 = (bf16[3,64,1024]{2,1,0:T(8,128)(2,1)}, bf16[3,64,1024]{2,1,0:T(8,128)(2,1)S(1)}, u32[]{:S(2)}, u32[]{:S(2)}) collective-permute-start(bf16[3,64,1024]{2,1,0:T(8,128)(2,1)} %get-tuple-element.299), channel_id=1, source_target_pairs={{0,1},{1,0},{2,3},{3,2},{4,5},{5,4},{6,7},{7,6},{8,9},{9,8},{10,11... | collective-permute-start | bytes 1179656 | tf_op jit(solution)/shard_map/ppermute | solution.py:38
  160.2 30.0 %collective-permute-start.49 = (bf16[3,64,1024]{2,1,0:T(8,128)(2,1)}, bf16[3,64,1024]{2,1,0:T(8,128)(2,1)S(1)}, u32[]{:S(2)}, u32[]{:S(2)}) collective-permute-start(bf16[3,64,1024]{2,1,0:T(8,128)(2,1)} %get-tuple-element.300), channel_id=1, source_target_pairs={{0,2},{1,3},{2,0},{3,1},{4,6},{5,7},{6,4},{7,5},{8,10},{9,11},{10,... | collective-permute-start | bytes 1179656 | tf_op jit(solution)/shard_map/ppermute | solution.py:38
  162.6 27.6 %collective-permute-start.50 = (bf16[3,64,1024]{2,1,0:T(8,128)(2,1)}, bf16[3,64,1024]{2,1,0:T(8,128)(2,1)S(1)}, u32[]{:S(2)}, u32[]{:S(2)}) collective-permute-start(bf16[3,64,1024]{2,1,0:T(8,128)(2,1)} %get-tuple-element.301), channel_id=1, source_target_pairs={{0,3},{1,2},{2,1},{3,0},{4,7},{5,6},{6,5},{7,4},{8,11},{9,10},{10,... | collective-permute-start | bytes 1179656 | tf_op jit(solution)/shard_map/ppermute | solution.py:38
  192.7 49.5 %collective-permute-start.61 = (bf16[3,256,1024]{2,1,0:T(8,128)(2,1)S(1)}, bf16[3,256,1024]{2,1,0:T(8,128)(2,1)S(1)}, u32[]{:S(2)}, u32[]{:S(2)}) collective-permute-start(bf16[3,256,1024]{2,1,0:T(8,128)(2,1)S(1)} %shard_map.108.refs_5_), channel_id=1, source_target_pairs={{0,16},{4,20},{8,24},{12,28},{16,0},{20,4},{24,8},{28,12},{1,17},{... | collective-permute-start | bytes 4718600 | tf_op jit(solution)/shard_map/ppermute | solution.py:38
  193.3 48.8 %collective-permute-start.60 = (bf16[3,256,1024]{2,1,0:T(8,128)(2,1)S(1)}, bf16[3,256,1024]{2,1,0:T(8,128)(2,1)S(1)}, u32[]{:S(2)}, u32[]{:S(2)}) collective-permute-start(bf16[3,256,1024]{2,1,0:T(8,128)(2,1)S(1)} %shard_map.108.refs_5_), channel_id=1, source_target_pairs={{0,8},{4,12},{8,0},{12,4},{16,24},{20,28},{24,16},{28,20},{1,9},{5... | collective-permute-start | bytes 4718600 | tf_op jit(solution)/shard_map/ppermute | solution.py:38
  194.7 22.6 %collective-permute-start.51 = (bf16[512,512]{1,0:T(8,128)(2,1)S(1)}, bf16[512,512]{1,0:T(8,128)(2,1)S(1)}, u32[]{:S(2)}, u32[]{:S(2)}) collective-permute-start(bf16[512,512]{1,0:T(8,128)(2,1)S(1)} %copy-done.50), channel_id=1, source_target_pairs={{3,2},{0,1},{7,6},{4,5},{11,10},{8,9},{15,14},{12,13},{19,18},{16,... | collective-permute-start | bytes 1572872 | tf_op jit(solution)/shard_map/ppermute | solution.py:121
  217.4 24.7 %collective-permute-start.54 = (bf16[512,512]{1,0:T(8,128)(2,1)S(1)}, bf16[512,512]{1,0:T(8,128)(2,1)S(1)}, u32[]{:S(2)}, u32[]{:S(2)}) collective-permute-start(bf16[512,512]{1,0:T(8,128)(2,1)S(1)} %add_convert_fusion.6), channel_id=1, source_target_pairs={{0,2},{1,3},{2,0},{3,1},{4,6},{5,7},{6,4},{7,5},{8,10},{9,11},{10,... | collective-permute-start | bytes 1572872 | tf_op jit(solution)/shard_map/ppermute | solution.py:38
  244.8 29.5 %collective-permute-start.59 = (bf16[3,256,1024]{2,1,0:T(8,128)(2,1)S(1)}, bf16[3,256,1024]{2,1,0:T(8,128)(2,1)S(1)}, u32[]{:S(2)}, u32[]{:S(2)}) collective-permute-start(bf16[3,256,1024]{2,1,0:T(8,128)(2,1)S(1)} %shard_map.108.refs_5_), channel_id=1, source_target_pairs={{0,4},{4,0},{8,12},{12,8},{16,20},{20,16},{24,28},{28,24},{1,5},{5... | collective-permute-start | bytes 4718600 | tf_op jit(solution)/shard_map/ppermute | solution.py:38
  245.2 26.6 %collective-permute-start.56 = (bf16[512,512]{1,0:T(8,128)(2,1)S(1)}, bf16[512,512]{1,0:T(8,128)(2,1)S(1)}, u32[]{:S(2)}, u32[]{:S(2)}) collective-permute-start(bf16[512,512]{1,0:T(8,128)(2,1)S(1)} %fusion.9.refs_0_), channel_id=1, source_target_pairs={{0,2},{1,3},{2,0},{3,1},{4,6},{5,7},{6,4},{7,5},{8,10},{9,11},{10,... | collective-permute-start | bytes 1572872 | tf_op jit(solution)/shard_map/ppermute | solution.py:38
  247.7 24.5 %collective-permute-start.55 = (bf16[512,512]{1,0:T(8,128)(2,1)S(1)}, bf16[512,512]{1,0:T(8,128)(2,1)S(1)}, u32[]{:S(2)}, u32[]{:S(2)}) collective-permute-start(bf16[512,512]{1,0:T(8,128)(2,1)S(1)} %fusion.9.refs_0_), channel_id=1, source_target_pairs={{0,1},{1,0},{2,3},{3,2},{4,5},{5,4},{6,7},{7,6},{8,9},{9,8},{10,11... | collective-permute-start | bytes 1572872 | tf_op jit(solution)/shard_map/ppermute | solution.py:38
  260.5 42.3 %collective-permute-start.64 = (bf16[3,256,1024]{2,1,0:T(8,128)(2,1)S(1)}, bf16[3,256,1024]{2,1,0:T(8,128)(2,1)S(1)}, u32[]{:S(2)}, u32[]{:S(2)}) collective-permute-start(bf16[3,256,1024]{2,1,0:T(8,128)(2,1)S(1)} %collective-permute-done.60.refs_7_), channel_id=1, source_target_pairs={{0,4},{4,0},{8,12},{12,8},{16,20},{20,16},{24,28},{28,24},{1,5},{5... | collective-permute-start | bytes 4718600 | tf_op jit(solution)/shard_map/ppermute | solution.py:38
  260.6 44.7 %collective-permute-start.65 = (bf16[3,256,1024]{2,1,0:T(8,128)(2,1)S(1)}, bf16[3,256,1024]{2,1,0:T(8,128)(2,1)}, u32[]{:S(2)}, u32[]{:S(2)}) collective-permute-start(bf16[3,256,1024]{2,1,0:T(8,128)(2,1)S(1)} %collective-permute-done.61.refs_9_), channel_id=1, source_target_pairs={{0,4},{4,0},{8,12},{12,8},{16,20},{20,16},{24,28},{28,24},{1,5},{5... | collective-permute-start | bytes 4718600 | tf_op jit(solution)/shard_map/ppermute | solution.py:38
  273.8 29.0 %collective-permute-start.66 = (bf16[3,128,1024]{2,1,0:T(8,128)(2,1)S(1)}, bf16[3,128,1024]{2,1,0:T(8,128)(2,1)S(1)}, u32[]{:S(2)}, u32[]{:S(2)}) collective-permute-start(bf16[3,128,1024]{2,1,0:T(8,128)(2,1)S(1)} %collective-permute-done.62.refs_11_), channel_id=1, source_target_pairs={{0,4},{4,0},{8,12},{12,8},{16,20},{20,16},{24,28},{28,24},{1,5},{5... | collective-permute-start | bytes 2359304 | tf_op jit(solution)/shard_map/ppermute | solution.py:38
  273.8 29.0 %collective-permute-start.67 = (bf16[3,128,1024]{2,1,0:T(8,128)(2,1)S(1)}, bf16[3,128,1024]{2,1,0:T(8,128)(2,1)S(1)}, u32[]{:S(2)}, u32[]{:S(2)}) collective-permute-start(bf16[3,128,1024]{2,1,0:T(8,128)(2,1)S(1)} %collective-permute-done.63.refs_12_), channel_id=1, source_target_pairs={{0,4},{4,0},{8,12},{12,8},{16,20},{20,16},{24,28},{28,24},{1,5},{5... | collective-permute-start | bytes 2359304 | tf_op jit(solution)/shard_map/ppermute | solution.py:38
  274.3 28.5 %collective-permute-start.58 = (bf16[512,512]{1,0:T(8,128)(2,1)S(1)}, bf16[512,512]{1,0:T(8,128)(2,1)S(1)}, u32[]{:S(2)}, u32[]{:S(2)}) collective-permute-start(bf16[512,512]{1,0:T(8,128)(2,1)S(1)} %collective-permute-done.56.refs_2_), channel_id=1, source_target_pairs={{2,3},{1,0},{6,7},{5,4},{10,11},{9,8},{14,15},{13,12},{18,19},{17,... | collective-permute-start | bytes 1572872 | tf_op jit(solution)/shard_map/ppermute | solution.py:114
  332.9 25.3 %collective-permute-start.71 = (bf16[512,512]{1,0:T(8,128)(2,1)S(1)}, bf16[512,512]{1,0:T(8,128)(2,1)S(1)}, u32[]{:S(2)}, u32[]{:S(2)}) collective-permute-start(bf16[512,512]{1,0:T(8,128)(2,1)S(1)} %add_convert_fusion.5), channel_id=1, source_target_pairs={{0,2},{1,3},{2,0},{3,1},{4,6},{5,7},{6,4},{7,5},{8,10},{9,11},{10,... | collective-permute-start | bytes 1572872 | tf_op jit(solution)/shard_map/ppermute | solution.py:38
  336.5 22.0 %collective-permute-start.70 = (bf16[512,512]{1,0:T(8,128)(2,1)S(1)}, bf16[512,512]{1,0:T(8,128)(2,1)S(1)}, u32[]{:S(2)}, u32[]{:S(2)}) collective-permute-start(bf16[512,512]{1,0:T(8,128)(2,1)S(1)} %copy-done.51), channel_id=1, source_target_pairs={{0,1},{1,0},{2,3},{3,2},{4,5},{5,4},{6,7},{7,6},{8,9},{9,8},{10,11... | collective-permute-start | bytes 1572872 | tf_op jit(solution)/shard_map/ppermute | solution.py:38
  360.6 24.6 %collective-permute-start.77 = (bf16[512,512]{1,0:T(8,128)(2,1)}, bf16[512,512]{1,0:T(8,128)(2,1)}, u32[]{:S(2)}, u32[]{:S(2)}) collective-permute-start(bf16[512,512]{1,0:T(8,128)(2,1)} %add_convert_fusion.4), channel_id=1, source_target_pairs={{0,24},{4,28},{8,16},{12,20},{16,8},{20,12},{24,0},{28,4},{1,25},{... | collective-permute-start | bytes 1572872 | tf_op jit(solution)/shard_map/ppermute | solution.py:38
  (60 other events, 876.9 us)
